TPU v7x, 256 devices: a whole 4x4x8 slice. The times are simulated.
256 devices in a mesh: ctx: 8 (over y, core), grp: 16 (over x_hi, z), tp: 2 (over x_lo).
Axes of the slice: x: 4 (x_hi: 2, x_lo: 2; x = x_hi * 2 + x_lo), y: 4, z: 8, core: 2. Of those that a mesh axis runs over, the one named last changes fastest.
Arguments:
- queries: bfloat16 [32, 1024, 4096], P(('grp', 'tp'), 'ctx'), may hold values from -32 to 32
- keys: bfloat16 [32, 1024, 1024], P(('grp', 'tp'), 'ctx'), may hold values from -6 to 6
- values: bfloat16 [32, 1024, 1024], P(('grp', 'tp'), 'ctx'), may hold values from -6 to 6
- documents: int32 [32, 1024], P(('grp', 'tp'), 'ctx'), may hold values from 0 to 7, never falling along the last dimension, each value on 1 to 512 neighbouring positions
- residual: bfloat16 [32, 1024, 4096], P(('grp', 'tp'), 'ctx'), may hold values from -6 to 6
- labels: int32 [32, 64], P(('grp', 'tp'), 'ctx'), may hold values from 0 to 127
- out_weight: bfloat16 [4096, 4096], P('ctx', ('grp', 'tp')), may hold values from -0.09375 to 0.09375
- norm_gain: bfloat16 [4096], P(('grp', 'tp')), may hold values from 0.25 to 1.75
- gate_weight: bfloat16 [4096, 14336], P('ctx', ('grp', 'tp')), may hold values from -0.09375 to 0.09375
- up_weight: bfloat16 [4096, 14336], P('ctx', ('grp', 'tp')), may hold values from -0.09375 to 0.09375
- down_weight: bfloat16 [14336, 4096], P(('grp', 'tp'), 'ctx'), may hold values from -0.046875 to 0.046875
- reward_weight: bfloat16 [4096], P(('grp', 'tp')), may hold values from -0.09375 to 0.09375
Outputs:
- attended: bfloat16 [32, 1024, 4096], P(('grp', 'tp'), 'ctx')
- labeled: bfloat16 [2048, 4096], P('ctx', ('grp', 'tp'))
- reward: float32 [2048], P('ctx')
All inputs are finite; a program needn't handle non-finite values.
Results may differ from a plain program's by a relative error of at most 0.006.
Values may be sent and summed in bfloat16 or wider, within the bound.
A program may use at most 128 MiB of HBM per device.

v0:
```python
import jax
import jax.numpy as jnp
from jax import lax
from jax.sharding import PartitionSpec as P

D = 4096
H = 32
KVH = 8
HD = 128


def add_rows(total, left, piece):
    return total + jnp.dot(left, piece, preferred_element_type=jnp.float32)


def per_device(
    queries,
    keys,
    values,
    documents,
    residual,
    labels,
    out_weight,
    norm_gain,
    gate_weight,
    up_weight,
    down_weight,
    reward_weight,
):
    count = queries.shape[1]
    group = H // KVH
    query_rows = queries[0].reshape(count, KVH, group, HD)
    my_start = lax.axis_index("ctx") * count
    query_pos = my_start + jnp.arange(count, dtype=jnp.int32)
    query_doc = documents[0]
    top = jnp.full((KVH, group, count), -1e30, jnp.float32)
    key_piece = lax.all_gather(keys, "ctx", axis=1, tiled=True)
    value_piece = lax.all_gather(values, "ctx", axis=1, tiled=True)
    doc_piece = lax.all_gather(documents, "ctx", axis=1, tiled=True)
    width = key_piece.shape[1]
    key_rows = key_piece[0].reshape(width, KVH, HD)
    value_rows = value_piece[0].reshape(width, KVH, HD)
    key_pos = jnp.arange(width, dtype=jnp.int32)
    score = jnp.einsum(
        "rkgd,skd->kgrs", query_rows, key_rows, preferred_element_type=jnp.float32
    ) * HD ** (-0.5)
    keep = (key_pos[None, :] <= query_pos[:, None]) & (doc_piece[0][None, :] == query_doc[:, None])
    score = jnp.where(keep, score, -1e30)
    newtop = jnp.maximum(top, jnp.max(score, axis=-1))
    weight = jnp.where(keep, jnp.exp(score - newtop[..., None]), 0.0)
    total = jnp.sum(weight, axis=-1)
    summed = jnp.einsum(
        "kgrs,skd->kgrd",
        weight.astype(jnp.bfloat16),
        value_rows,
        preferred_element_type=jnp.float32,
    )
    top, total, summed = (newtop, total, summed)
    attended_rows = (
        jnp.transpose(summed / total[..., None], (2, 0, 1, 3))
        .reshape(count, D)
        .astype(jnp.bfloat16)
    )
    lab = labels[0]
    picked = attended_rows[lab]
    base = residual[0][lab]
    all_picked, all_base = (
        lax.all_gather(picked, ("grp", "tp"), axis=0, tiled=True),
        lax.all_gather(base, ("grp", "tp"), axis=0, tiled=True),
    )
    width = out_weight.shape[1]
    col_start = lax.axis_index(("grp", "tp")) * width
    base_cols = lax.dynamic_slice_in_dim(all_base, col_start, width, 1).astype(jnp.float32)
    state = add_rows(base_cols, all_picked, lax.all_gather(out_weight, "ctx", axis=0, tiled=True))
    squares = lax.psum(jnp.sum(state * state, axis=-1), ("grp", "tp"))
    scale_rows = lax.rsqrt(squares / D + 1e-05)
    normed_cols = (state * scale_rows[:, None] * norm_gain.astype(jnp.float32)[None, :]).astype(
        jnp.bfloat16
    )
    normed = lax.all_gather(normed_cols, ("grp", "tp"), axis=1, tiled=True)
    empty = jnp.zeros((normed.shape[0], gate_weight.shape[1]), jnp.float32)

    def add_one(total_rows, piece):
        return add_rows(total_rows, normed, piece)

    gate = add_one(empty, lax.all_gather(gate_weight, "ctx", axis=0, tiled=True))
    up = add_one(empty, lax.all_gather(up_weight, "ctx", axis=0, tiled=True))
    hidden = (jax.nn.silu(gate) * up).astype(jnp.bfloat16)
    terms = jnp.dot(
        hidden,
        lax.all_gather(down_weight, "ctx", axis=1, tiled=True),
        preferred_element_type=jnp.float32,
    )
    branch_cols = lax.psum_scatter(terms, ("grp", "tp"), scatter_dimension=1, tiled=True)
    labeled = (state + branch_cols).astype(jnp.bfloat16)
    partial_reward = jnp.dot(labeled, reward_weight, preferred_element_type=jnp.float32)
    reward = lax.psum(partial_reward, ("grp", "tp"))
    return (attended_rows[None], labeled, reward)


def solution(mesh):
    return jax.shard_map(
        per_device,
        mesh=mesh,
        in_specs=(
            P(("grp", "tp"), "ctx", None),
            P(("grp", "tp"), "ctx", None),
            P(("grp", "tp"), "ctx", None),
            P(("grp", "tp"), "ctx"),
            P(("grp", "tp"), "ctx", None),
            P(("grp", "tp"), "ctx"),
            P("ctx", ("grp", "tp")),
            P(("grp", "tp")),
            P("ctx", ("grp", "tp")),
            P("ctx", ("grp", "tp")),
            P(("grp", "tp"), "ctx"),
            P(("grp", "tp")),
        ),
        out_specs=(P(("grp", "tp"), "ctx", None), P("ctx", ("grp", "tp")), P("ctx")),
        check_vma=False,
    )
```

profile of v0, /device:TPU:24, one launch (start us, length us, event | category | flops | bytes accessed | tf_op | source)
XLA Modules:
  0.0 918.8 jit_solution(1755503984856011001)
XLA Ops:
  7.2 1.9 copy.33
  9.1 0.0 all-gather.14.cloned.1.call-start
  9.2 0.7 all-gather.14.cloned.1.call-update
  9.9 0.0 all-gather.26.cloned.1.call-start
  9.9 0.7 fusion.20
  10.6 1.2 gather_fusion
  11.8 0.0 all-gather.16.cloned.1.call-start
  11.9 0.5 all-gather.16.cloned.1.call-update
  12.4 0.0 all-gather.28.cloned.1.call-start
  12.5 8.7 all_gather.30
  21.1 1.8 reshape_squeeze.10
  22.9 0.2 fusion.13
  23.2 19.1 %all-gather.12.cloned.1.call-done = bf16[1,1024,1024]{1,2,0:T(8,128)(2,1)} async-done(((bf16[1,128,1024]{1,2,0:T(8,128)(2,1)}), bf16[1,1024,1024]{1,2,0:T(8,128)(2,1)}) %all-gather.12.cloned.1.call-update) | async-done | bytes 2097168 | tf_op jit(solution)/shard_map/all_gather | solution.py:37
  42.3 4.4 fusion
  46.7 5.7 copy-done.1
  52.4 4.1 fusion.1
  56.6 16.1 %all-gather.14.cloned.1.call-done = bf16[1,1024,1024]{2,1,0:T(8,128)(2,1)} async-done(((bf16[1,128,1024]{2,1,0:T(8,128)(2,1)}), bf16[1,1024,1024]{2,1,0:T(8,128)(2,1)}) %all-gather.14.cloned.1.call-update) | async-done | bytes 2097168 | tf_op jit(solution)/shard_map/all_gather | solution.py:38
  72.6 3.9 copy.36
  76.6 10.5 %fusion.6 = bf16[128,8,4,128]{0,3,2,1:T(8,128)(2,1)S(1)} fusion(bf16[1024,8,128,1]{0,2,3,1:T(8,128)(2,1)} %bitcast.55, f32[8,1024,128,4]{2,1,3,0:T(8,128)} %copy-done.1, f32[8,4,128]{2,1,0:T(4,128)S(1)} %broadcast_maximum_fusion, pred[128,1024]{0,1:T(8,128)(4,1)S(1)} %fusion.13, f32[128,8,4]{0,2,1:T(4,128)S(1)} %bitcast.57), kind=kOutput, calls=%fused_computation.10 | convolution fusion | flops 1095761920 | bytes 20086784 | tf_op jit(solution)/shard_map/kgrs,skd->kgrd/dot_general | solution.py:52
  87.0 0.5 copy.39
  87.6 1.2 gather_fusion.1
  88.8 0.0 all-gather.20.cloned.1.call-start
  88.9 0.5 all-gather.20.cloned.1.call-update
  89.4 0.0 all-gather.18.cloned.1.call-start
  89.5 129.7 %all-gather.26.cloned.1.call-done = bf16[256,4096]{1,0:T(8,128)(2,1)} async-done(((bf16[8,4096]{1,0:T(8,128)(2,1)}), bf16[256,4096]{1,0:T(8,128)(2,1)}) %all-gather.26.cloned.1.call-update) | async-done | bytes 2097168 | tf_op jit(solution)/shard_map/all_gather | solution.py:69
  219.1 0.8 constant_dynamic-slice_fusion
  220.0 0.1 copy.49
  220.1 23.0 %all-gather.16.cloned.1.call-done = bf16[4096,128]{1,0:T(8,128)(2,1)} async-done(((bf16[512,128]{1,0:T(8,128)(2,1)}), bf16[4096,128]{1,0:T(8,128)(2,1)}) %all-gather.16.cloned.1.call-update) | async-done | bytes 1048592 | tf_op jit(solution)/shard_map/all_gather | solution.py:74
  243.1 147.2 %all-gather.28.cloned.1.call-done = bf16[256,4096]{1,0:T(8,128)(2,1)} async-done(((bf16[8,4096]{1,0:T(8,128)(2,1)}), bf16[256,4096]{1,0:T(8,128)(2,1)}) %all-gather.28.cloned.1.call-update) | async-done | bytes 2097168 | tf_op jit(solution)/shard_map/all_gather | solution.py:68
  390.3 2.7 multiply_reduce_fusion
  393.0 74.5 %psum.14 = f32[256]{0:T(256)S(1)} all-reduce(f32[256]{0:T(256)S(1)} %get-tuple-element.14), channel_id=1, replica_groups=mesh['ctx'=8,'grp'=16,'tp'=2] {'grp','tp'}, use_global_device_ids=true, to_apply=%region_3.4 | all-reduce | flops 256 | bytes 2048 | tf_op jit(solution)/shard_map/psum | solution.py:75
  467.5 0.7 multiply_convert_fusion
  468.2 0.0 all-gather.22.cloned.1.call-start
  468.2 0.7 all-gather.22.cloned.1.call-update
  469.0 0.0 all-gather.24.cloned.1.call-start
  469.0 0.7 all-gather.24.cloned.1.call-update
  469.7 0.2 reduce-scatter.2.cloned.1.call-start
  469.9 135.5 %all-gather.18.cloned.1.call-done = bf16[256,4096]{0,1:T(8,128)(2,1)} async-done(((bf16[256,128]{0,1:T(8,128)(2,1)}), bf16[256,4096]{0,1:T(8,128)(2,1)}) %all-gather.18.cloned.1.call-update) | async-done | bytes 2097168 | tf_op jit(solution)/shard_map/all_gather | solution.py:80
  605.4 3.8 fusion.27
  609.3 26.8 %all-gather.22.cloned.1.call-done = bf16[4096,448]{0,1:T(8,128)(2,1)} async-done(((bf16[512,448]{0,1:T(8,128)(2,1)}), bf16[4096,448]{0,1:T(8,128)(2,1)}) %all-gather.22.cloned.1.call-update) | async-done | bytes 3670032 | tf_op jit(solution)/shard_map/all_gather | solution.py:87
  636.0 34.3 %all-gather.24.cloned.1.call-done = bf16[448,4096]{1,0:T(8,128)(2,1)} async-done(((bf16[448,512]{1,0:T(8,128)(2,1)}), bf16[448,4096]{1,0:T(8,128)(2,1)}) %all-gather.24.cloned.1.call-update) | async-done | bytes 3670032 | tf_op jit(solution)/shard_map/all_gather | solution.py:91
  670.3 9.8 %fusion.12 = f32[256,4096]{0,1:T(8,128)} fusion(bf16[448,4096]{1,0:T(8,128)(2,1)} %all-gather.24.cloned.1.call-done, bf16[4096,448]{0,1:T(8,128)(2,1)} %all-gather.22.cloned.1.call-done, bf16[256,4096]{0,1:T(8,128)(2,1)} %all-gather.18.cloned.1.call-done, f32[256,448]{0,1:T(8,128)S(1)} %fusion.27), kind=kOutput, calls=%fused_computation.16 | convolution fusion | flops 1879736320 | bytes 14090240 | tf_op jit(solution)/shard_map/dot_general | solution.py:89
  680.2 1.3 copy.41
  681.5 157.5 %reduce-scatter.2.cloned.1.call-done = f32[256,128]{0,1:T(8,128)} async-done(((f32[256,4096]{0,1:T(8,128)}), f32[256,128]{0,1:T(8,128)}) %reduce-scatter.2.cloned.1.call-update) | async-done | bytes 131088 | tf_op jit(solution)/shard_map/reduce_scatter | solution.py:94
  839.0 0.9 add_convert_fusion
  839.9 0.7 copy.42
  840.6 0.1 fusion.21
  840.7 71.3 %psum.15 = f32[256]{0:T(256)} all-reduce(f32[256]{0:T(256)S(1)} %bitcast.58), channel_id=1, replica_groups=mesh['ctx'=8,'grp'=16,'tp'=2] {'grp','tp'}, use_global_device_ids=true, to_apply=%region_5.6 | all-reduce | flops 256 | bytes 2048 | tf_op jit(solution)/shard_map/psum | solution.py:97
  (21 shorter events, 0.2 us)
Async XLA Ops:
  7.2 3.4 copy-start
  7.2 15.8 %copy-start.2 = (s32[1,128]{1,0:T(1,128)S(1)}, s32[1,128]{1,0:T(1,128)}, u32[]{:S(2)}) copy-start(s32[1,128]{1,0:T(1,128)} %param.15) | copy-start | bytes 1540
  7.2 35.1 %all-gather.12.cloned.1.call-start = ((), (), s32[]{:S(2)}) async-start(), calls=%async_computation.1 | async-start | bytes 2359296 | tf_op jit(solution)/shard_map/all_gather | solution.py:37
  9.1 63.5 %all-gather.14.cloned.1.call-start = ((), (), s32[]{:S(2)}) async-start(), calls=%async_computation.2 | async-start | bytes 2359296 | tf_op jit(solution)/shard_map/all_gather | solution.py:38
  9.9 209.3 %all-gather.26.cloned.1.call-start = ((), (), s32[]{:S(2)}) async-start(), calls=%async_computation.9 | async-start | bytes 2162688 | tf_op jit(solution)/shard_map/all_gather | solution.py:69
  11.8 231.2 %all-gather.16.cloned.1.call-start = ((), (), s32[]{:S(2)}) async-start(), calls=%async_computation.3 | async-start | bytes 1179648 | tf_op jit(solution)/shard_map/all_gather | solution.py:74
  12.4 377.9 %all-gather.28.cloned.1.call-start = ((), (), s32[]{:S(2)}) async-start(), calls=%async_computation.10 | async-start | bytes 2162688 | tf_op jit(solution)/shard_map/all_gather | solution.py:68
  46.7 5.7 copy-start.1
  76.6 12.9 %copy-start.4 = (bf16[128]{0:T(256)(128)(2,1)S(1)}, bf16[128]{0:T(256)(128)(2,1)}, u32[]{:S(2)}) copy-start(bf16[128]{0:T(256)(128)(2,1)} %param.19) | copy-start | bytes 772
  88.8 381.1 %all-gather.20.cloned.1.call-start = ((), (), s32[]{:S(2)}) async-start(), calls=%async_computation.5 | async-start | bytes 4128768 | tf_op jit(solution)/shard_map/all_gather | solution.py:86
  89.4 516.0 %all-gather.18.cloned.1.call-start = ((), (), s32[]{:S(2)}) async-start(), calls=%async_computation.4 | async-start | bytes 2162688 | tf_op jit(solution)/shard_map/all_gather | solution.py:80
  468.2 167.8 %all-gather.22.cloned.1.call-start = ((), (), s32[]{:S(2)}) async-start(), calls=%async_computation.6 | async-start | bytes 4128768 | tf_op jit(solution)/shard_map/all_gather | solution.py:87
  469.0 201.4 %all-gather.24.cloned.1.call-start = ((), (), s32[]{:S(2)}) async-start(), calls=%async_computation.7 | async-start | bytes 4128768 | tf_op jit(solution)/shard_map/all_gather | solution.py:91
  469.7 369.3 %reduce-scatter.2.cloned.1.call-start = ((), (), s32[]{:S(2)}) async-start(), calls=%async_computation.8 | async-start | bytes 4325376 | tf_op jit(solution)/shard_map/reduce_scatter | solution.py:94
  680.2 160.5 %copy-start.3 = (bf16[128]{0:T(256)(128)(2,1)S(1)}, bf16[128]{0:T(256)(128)(2,1)}, u32[]{:S(2)}) copy-start(bf16[128]{0:T(256)(128)(2,1)} %param.23) | copy-start | bytes 772
Sparse Core Ops, SparseCore 0:
  10.4 31.8 all-gather.11
  44.1 28.4 all-gather.13
  74.4 144.6 all-gather.25
  220.9 22.1 all-gather.15
  245.3 144.9 all-gather.27
  392.0 28.7 all-gather.19
  468.3 137.0 all-gather.17
  607.3 28.6 all-gather.21
  637.9 32.4 all-gather.23
  680.3 158.6 reduce-scatter.1
where the time goes:
time: 920 us; the launch traced here: 919 us
  waiting for transfers between devices  692 us (75%)
  blocking collectives  154 us (17%)
  matrix products  31.3 us (3%)
  local copies, waits for them, and re-layouts  19.3 us (2%)
  between operations  14.3 us (2%)
    reduce_scatter x1, waiting for transfers between devices, per_device(): lax.psum_scatter(terms, ('grp', 'tp'), scatter_dimension=1, tiled=True)  157 us
    all_gather x1, waiting for transfers between devices, per_device(): lax.all_gather(picked, ('grp', 'tp'), axis=0, tiled=True)  147 us
    all_gather x1, waiting for transfers between devices, per_device(): normed = lax.all_gather(normed_cols, ('grp', 'tp'), axis=1, tiled=True)  135 us
    all_gather x1, waiting for transfers between devices, per_device(): lax.all_gather(base, ('grp', 'tp'), axis=0, tiled=True)  130 us
    psum x1, blocking collectives, per_device(): squares = lax.psum(jnp.sum(state * state, axis=-1), ('grp', 'tp'))  74.5 us
    psum x1, blocking collectives, per_device(): reward = lax.psum(partial_reward, ('grp', 'tp'))  71.3 us
    all_gather x1, waiting for transfers between devices, per_device(): lax.all_gather(down_weight, 'ctx', axis=1, tiled=True)  34.3 us
    all_gather x1, waiting for transfers between devices, per_device(): up = add_one(empty, lax.all_gather(up_weight, 'ctx', axis=0, tiled=True))  26.8 us
  transfers between devices with their start and end apart: 10, of which 9 were waited for; matrix products, arithmetic and copies ran while one was open for 4% of the time, Pallas kernels for 0%

commit v1 on v0

v1 whole, which is shorter than its diff:
```python
import functools
import math

import jax
import jax.numpy as jnp
from jax import lax
from jax.experimental import pallas as pl
from jax.experimental.pallas import tpu as pltpu
from jax.sharding import PartitionSpec as P

MESH = pl.DeviceIdType.MESH
NX, NY, NZ = 4, 4, 8
D, H, KVH, HD, FF = 4096, 32, 8, 128, 14336
TOK, LAB = 128, 8
ROWS = 256
FFL = 448
F32, BF16 = jnp.float32, jnp.bfloat16
SCALE2 = HD**-0.5 * math.log2(math.e)
NSEM = 176


def block_of(col):
    grp, tp = col // 2, col % 2
    return (grp // NZ) * 2 + tp, grp % NZ


def nt(a, b):
    return lax.dot_general(a, b, (((1,), (1,)), ((), ())), preferred_element_type=F32)


def body(
    q_ref,
    k_ref,
    v_ref,
    doc_ref,
    res_ref,
    lab_ref,
    ow_ref,
    gain_ref,
    gate_ref,
    up_ref,
    dn_ref,
    rw_ref,
    att_ref,
    labeled_ref,
    reward_ref,
    kbuf,
    vbuf,
    dbuf,
    ow,
    gu,
    dn,
    bias,
    qlab,
    plab,
    a0,
    a1,
    bsrc,
    bz,
    bx,
    state,
    s0,
    s1,
    acc,
    tb0,
    rx0,
    sb0,
    rz0,
    tb1,
    rp,
    rm,
    sp,
    sm,
    sb1,
    rx1,
    prx,
    prz,
    ss,
    rs,
    ls,
):
    ctx, grp, tp = lax.axis_index("ctx"), lax.axis_index("grp"), lax.axis_index("tp")
    y, core = ctx // 2, ctx % 2
    x, z = (grp // NZ) * 2 + tp, grp % NZ
    other = y * 2 + 1 - core

    def wrap(v, n):
        return lax.rem(v + n, n)

    def dev(axis, k):
        if axis == "y":
            return {"ctx": wrap(y + k, NY) * 2 + core}
        if axis == "core":
            return {"ctx": other}
        if axis == "z":
            return {"grp": (x // 2) * NZ + wrap(z + k, NZ)}
        there = wrap(x + k, NX)
        return {"grp": (there // 2) * NZ + z, "tp": there % 2}

    ids = iter(range(NSEM))
    sent = []

    def send(src, dst, axis, k, cond=None):
        i = next(ids)
        copy = pltpu.make_async_remote_copy(
            src_ref=src,
            dst_ref=dst,
            send_sem=ss.at[i],
            recv_sem=rs.at[i],
            device_id=dev(axis, k),
            device_id_type=MESH,
        )
        if cond is None:
            copy.start()
        else:
            pl.when(cond)(copy.start)
        sent.append((copy, cond))
        return i

    def recv(dst, i):
        pltpu.make_async_remote_copy(
            src_ref=dst,
            dst_ref=dst,
            send_sem=ss.at[i],
            recv_sem=rs.at[i],
            device_id={"ctx": other},
            device_id_type=MESH,
        ).wait_recv()

    barrier = pltpu.get_barrier_semaphore()
    partners = [("core", 1)]
    partners += [("y", k) for k in range(1, NY)]
    partners += [("x", k) for k in range(1, NX)]
    partners += [("z", k) for k in range(1, NZ)]
    for axis, k in partners:
        pl.semaphore_signal(barrier, inc=1, device_id=dev(axis, k), device_id_type=MESH)

    local = [
        pltpu.make_async_copy(k_ref.at[0], kbuf.at[ctx], ls.at[0]),
        pltpu.make_async_copy(v_ref.at[0], vbuf.at[ctx], ls.at[1]),
        pltpu.make_async_copy(ow_ref, ow.at[ctx], ls.at[2]),
        pltpu.make_async_copy(dn_ref, dn.at[ctx], ls.at[3]),
    ]
    for copy in local:
        copy.start()
    dbuf[ctx] = jnp.broadcast_to(doc_ref[...], (8, TOK))
    for j in range(1, 2 * NY):

        @pl.when(j > ctx)
        def _():
            kbuf[j] = jnp.zeros_like(kbuf[j])
            vbuf[j] = jnp.zeros_like(vbuf[j])
            dbuf[j] = jnp.zeros_like(dbuf[j])

    pl.semaphore_wait(barrier, len(partners))

    kv_ids = {}
    for k in (1, 3, 2):
        ok = y + k < NY
        kv_ids[k] = [
            send(dbuf.at[ctx], dbuf.at[ctx], "y", k, ok),
            send(k_ref.at[0], kbuf.at[ctx], "y", k, ok),
            send(v_ref.at[0], vbuf.at[ctx], "y", k, ok),
        ]
    first = core == 0
    kv_own = [
        send(dbuf.at[ctx], dbuf.at[ctx], "core", 1, first),
        send(k_ref.at[0], kbuf.at[ctx], "core", 1, first),
        send(v_ref.at[0], vbuf.at[ctx], "core", 1, first),
    ]

    def w_start(src, buf):
        half = buf.shape[1] // 2

        def part(h):
            return src.at[pl.ds(h * half, half)]

        def slot(h):
            return buf.at[ctx, pl.ds(h * half, half)]

        got = {}
        got["up", 0] = send(part(0), slot(0), "y", 1)
        got["dn", 1] = send(part(1), slot(1), "y", -1)
        got["up", 1] = send(part(1), slot(1), "y", 1)
        got["dn", 0] = send(part(0), slot(0), "y", -1)
        got["own"] = send(src, buf.at[ctx], "core", 1)
        return got

    def w_piece(buf, k, h, c):
        half = buf.shape[1] // 2
        return buf.at[wrap(y + k, NY) * 2 + c, pl.ds(h * half, half)]

    def w_turn(buf, got):
        for name, h, k in (("up", 0, -1), ("dn", 1, 1)):
            ref = w_piece(buf, k, h, core)
            recv(ref, got[name, h])
            got["far", h] = send(ref, ref, "y", -k)
            got["core", k, h] = send(ref, ref, "core", 1)

    def w_share(buf, got):
        for name, h, k in (("up", 1, -1), ("dn", 0, 1)):
            ref = w_piece(buf, k, h, core)
            recv(ref, got[name, h])
            got["core", k, h] = send(ref, ref, "core", 1)
        for h in (0, 1):
            ref = w_piece(buf, 2, h, core)
            recv(ref, got["far", h])
            got["core", 2, h] = send(ref, ref, "core", 1)

    def w_done(buf, got):
        recv(buf.at[other], got["own"])
        for k in (-1, 1, 2):
            for h in (0, 1):
                recv(w_piece(buf, k, h, 1 - core), got["core", k, h])

    ow_got = w_start(ow_ref, ow)
    gu[ctx, :, :FFL] = gate_ref[...]
    gu[ctx, :, FFL:] = up_ref[...]
    gu_got = w_start(gu.at[ctx], gu)
    dn_got = w_start(dn_ref, dn)

    row_of = lax.broadcasted_iota(jnp.int32, (LAB, TOK), 0)
    lane_of = lax.broadcasted_iota(jnp.int32, (LAB, TOK), 1)
    lab_col = jnp.zeros((LAB, TOK), jnp.int32)
    for r in range(LAB):
        lab_col = jnp.where(row_of == r, lab_ref[0, r], lab_col)
    chosen = (lane_of == lab_col).astype(F32)
    pick = chosen.astype(BF16)

    base = jnp.dot(pick, res_ref[0], preferred_element_type=F32)
    for col in range(NX * NZ):
        bx_, bz_ = block_of(col)
        bsrc[bz_, bx_] = base[:, col * HD : (col + 1) * HD]
    bz[z] = bsrc[z]
    bz_ids = {k: send(bsrc.at[wrap(z + k, NZ)], bz.at[z], "z", k) for k in range(1, NZ)}

    q_lab = jnp.dot(pick, q_ref[0], preferred_element_type=F32).astype(BF16)
    for k in range(KVH):
        qlab[k] = jnp.concatenate(
            [q_lab[:, (4 * k + g) * HD : (4 * k + g + 1) * HD] for g in range(4)], axis=0
        )

    for k in range(1, NZ):
        recv(bz.at[wrap(z - k, NZ)], bz_ids[k])
    bx[x] = bz[:, x]
    bx_ids = {k: send(bz.at[:, wrap(x + k, NX)], bx.at[x], "x", k) for k in range(1, NX)}

    for copy in local:
        copy.wait()

    bufs = (dbuf, kbuf, vbuf)
    kv_core = {}
    for k in (1, 3, 2):
        ok = y - k >= 0
        src = wrap(y - k, NY) * 2 + core

        @pl.when(ok)
        def _(k=k, src=src):
            for buf, i in zip(bufs, kv_ids[k]):
                recv(buf.at[src], i)

        kv_core[k] = [send(buf.at[src], buf.at[src], "core", 1, ok) for buf in bufs]
    for k in (1, 3, 2):
        src = wrap(y - k, NY) * 2 + 1 - core

        @pl.when(y - k >= 0)
        def _(k=k, src=src):
            for buf, i in zip(bufs, kv_core[k]):
                recv(buf.at[src], i)

    @pl.when(core == 1)
    def _():
        for buf, i in zip(bufs, kv_own):
            recv(buf.at[other], i)

    key_doc = jnp.concatenate([dbuf[j][0:1] for j in range(2 * NY)], axis=1).astype(F32)
    key_pos = lax.broadcasted_iota(jnp.int32, (1, 2 * NY * TOK), 1)
    my_doc = doc_ref[...].astype(F32)

    lab_doc = jnp.sum(chosen * my_doc, axis=1, keepdims=True)
    lab_pos = lab_col[:, 0:1] + ctx * TOK
    keep = (key_pos <= lab_pos) & (key_doc == lab_doc)
    lab_bias = jnp.where(keep, 0.0, -1e30)
    lab_bias = jnp.concatenate([lab_bias] * 4, axis=0)

    def attend(q, k, add):
        lanes = pl.ds(pl.multiple_of(k * HD, HD), HD)
        keys = kbuf[:, :, lanes].reshape(2 * NY * TOK, HD)
        values = vbuf[:, :, lanes].reshape(2 * NY * TOK, HD)
        score = nt(q, keys) * SCALE2 + add
        weight = jnp.exp2(score - jnp.max(score, axis=1, keepdims=True))
        total = jnp.sum(weight, axis=1, keepdims=True)
        return jnp.dot(weight.astype(BF16), values, preferred_element_type=F32) / total

    def lab_head(k, carry):
        plab[k] = attend(qlab[k], k, lab_bias)
        return carry

    lax.fori_loop(0, KVH, lab_head, 0)
    halves = []
    for h in range(2):
        rows = []
        for sub in range(2):
            pieces = []
            for k in (4 * h + 2 * sub, 4 * h + 2 * sub + 1):
                pieces += [plab[k, g * LAB : (g + 1) * LAB] for g in range(4)]
            rows.append(jnp.concatenate(pieces, axis=1))
        halves.append(jnp.concatenate(rows, axis=0).astype(BF16))
    a0[x, z] = halves[0]
    a1[z, x] = halves[1]

    def gather_start(b0, b1):
        return (
            {k: send(b1.at[z, x], b1.at[z, x], "x", k) for k in range(1, NX)},
            {k: send(b0.at[x, z], b0.at[x, z], "z", k) for k in range(1, NZ)},
        )

    def gather_rest(b0, b1, started, between):
        x_ids, z_ids = started
        for k in range(1, NX):
            recv(b1.at[z, wrap(x - k, NX)], x_ids[k])
        up = send(b1.at[z], b1.at[z], "z", 1)
        down = send(b1.at[z], b1.at[z], "z", -1)
        for k in range(1, NZ):
            recv(b0.at[x, wrap(z - k, NZ)], z_ids[k])
        far = {k: send(b0.at[x], b0.at[x], "x", k) for k in (1, 3, 2)}
        lo, hi = pl.ds(0, NX // 2), pl.ds(NX // 2, NX // 2)
        for step in range(1, 4):
            between(step)
            from_low, from_high = wrap(z - step, NZ), wrap(z + step, NZ)
            recv(b1.at[from_low], up)
            part = b1.at[from_low] if step < 3 else b1.at[from_low, lo]
            up = send(part, part, "z", 1)
            recv(b1.at[from_high], down)
            part = b1.at[from_high] if step < 3 else b1.at[from_high, hi]
            down = send(part, part, "z", -1)
        between(4)
        recv(b1.at[wrap(z + 4, NZ), lo], up)
        recv(b1.at[wrap(z + 4, NZ), hi], down)
        for k in (1, 3, 2):
            recv(b0.at[wrap(x - k, NX)], far[k])

    def make_bias():
        doc_col = jnp.transpose(jnp.broadcast_to(my_doc, (TOK, TOK)))[:, 0:1]
        my_pos = lax.broadcasted_iota(jnp.int32, (TOK, 1), 0) + ctx * TOK
        full = (key_pos <= my_pos) & (key_doc == doc_col)
        bias[...] = jnp.where(full, 0.0, -1e30)

    def att_heads(start, stop):
        def one(h, carry):
            lanes = pl.ds(pl.multiple_of(h * HD, HD), HD)
            out = attend(q_ref[0, :, lanes], h // 4, bias[...])
            att_ref[0, :, lanes] = out.astype(BF16)
            return carry

        lax.fori_loop(start, stop, one, 0)

    started = gather_start(a0, a1)
    make_bias()
    w_turn(ow, ow_got)
    w_share(ow, ow_got)
    for k in range(1, NX):
        recv(bx.at[wrap(x - k, NX)], bx_ids[k])

    def between_first(step):
        att_heads(4 * step - 4, 4 * step)

    gather_rest(a0, a1, started, between_first)
    w_done(ow, ow_got)

    whole = ow[...].reshape(D, HD)
    quarter = D // 4
    flat = {0: a0[...].reshape(-1, quarter), 1: a1[...].reshape(-1, quarter)}
    proj = []
    for h in range(2):
        wide = jnp.concatenate(
            [whole[(2 * h + s) * quarter : (2 * h + s + 1) * quarter] for s in range(2)], axis=1
        )
        proj.append(jnp.dot(flat[h], wide, preferred_element_type=F32))
    for col in range(NX * NZ):
        bx_, bz_ = block_of(col)
        r0, r1 = (bx_ * NZ + bz_) * 16, (bz_ * NX + bx_) * 16
        state[col * LAB : (col + 1) * LAB] = (
            bx[bx_, bz_]
            + (proj[0][r0 : r0 + 8, :HD] + proj[0][r0 + 8 : r0 + 16, HD:])
            + (proj[1][r1 : r1 + 8, :HD] + proj[1][r1 + 8 : r1 + 16, HD:])
        )

    gain = gain_ref[...].astype(F32)
    sixteen = lax.broadcasted_iota(jnp.int32, (16, HD), 0)
    for h, put in ((0, s0.at[x, z]), (1, s1.at[z, x])):
        part = state[h * 128 : (h + 1) * 128]
        put[0:128] = (part * gain).astype(BF16)
        square = jnp.sum(jnp.transpose(part * part), axis=0, keepdims=True)
        top = square.astype(BF16).astype(F32)
        mid = (square - top).astype(BF16).astype(F32)
        low = square - top - mid
        put[128:144] = jnp.where(
            sixteen == 0,
            top,
            jnp.where(sixteen == 1, mid, jnp.where(sixteen == 2, low, 0.0)),
        ).astype(BF16)

    started = gather_start(s0, s1)
    w_turn(gu, gu_got)
    w_turn(dn, dn_got)

    def between_second(step):
        att_heads(12 + 4 * step, 16 + 4 * step)

    gather_rest(s0, s1, started, between_second)
    w_share(gu, gu_got)
    w_done(gu, gu_got)

    def inv_rms(buf):
        total = jnp.zeros((16, HD), F32)
        for i in range(buf.shape[0]):
            for j in range(buf.shape[1]):
                total = total + buf[i, j, 128:144].astype(F32)
        line = jnp.sum(total, axis=0, keepdims=True)
        col = jnp.transpose(jnp.broadcast_to(line, (128, 128)))
        return lax.rsqrt(col / D + 1e-5)

    scale = jnp.concatenate([inv_rms(s0), inv_rms(s1)], axis=0)
    acc[...] = jnp.zeros_like(acc)
    for c in range(2 * NY):
        pieces = []
        for col in range(4 * c, 4 * c + 4):
            bx_, bz_ = block_of(col)
            pieces.append(jnp.concatenate([s0[bx_, bz_, 0:128], s1[bz_, bx_, 0:128]], axis=0))
        acc[...] += jnp.dot(jnp.concatenate(pieces, axis=1), gu[c], preferred_element_type=F32)
    scale = jnp.concatenate([scale] * 4, axis=1)[:, :FFL]
    gate = acc[:, :FFL] * scale
    up = acc[:, FFL:] * scale
    hidden = (gate / (1.0 + jnp.exp(-gate)) * up).astype(BF16)

    w_share(dn, dn_got)
    w_done(dn, dn_got)
    for c in range(2 * NY):
        terms = jnp.dot(hidden, dn[c], preferred_element_type=F32)
        for i in range(4):
            bx_, bz_ = block_of(4 * c + i)
            cols = terms[:, i * HD : (i + 1) * HD]
            tb0[bx_, bz_] = cols[:128].astype(BF16)
            tb1[bz_, bx_] = cols[128:].astype(BF16)

    x_ids = {k: send(tb0.at[wrap(x + k, NX)], rx0.at[x], "x", k) for k in (1, 3, 2)}
    p_id = send(tb1.at[wrap(z + 4, NZ)], rp.at[0], "z", 1)
    m_id = send(tb1.at[wrap(z - 3, NZ)], rm.at[0], "z", -1)
    for step in range(3):
        recv(rp.at[step], p_id)
        sp[step] = (rp[step].astype(F32) + tb1[wrap(z + 3 - step, NZ)].astype(F32)).astype(BF16)
        p_id = send(sp.at[step], rp.at[step + 1], "z", 1)
        if step < 2:
            recv(rm.at[step], m_id)
            sm[step] = (rm[step].astype(F32) + tb1[wrap(z - 2 + step, NZ)].astype(F32)).astype(BF16)
            m_id = send(sm.at[step], rm.at[step + 1], "z", -1)
    for k in (1, 3, 2):
        recv(rx0.at[wrap(x - k, NX)], x_ids[k])

    def add_x(i):
        total = tb0[x, i].astype(F32)
        for k in (1, 2, 3):
            total = total + rx0[wrap(x - k, NX), i].astype(F32)
        return total

    def put_x(i, carry):
        sb0[i] = add_x(i).astype(BF16)
        return carry

    lax.fori_loop(0, NZ, put_x, 0)
    z_ids = {k: send(sb0.at[wrap(z + k, NZ)], rz0.at[z], "z", k) for k in range(1, NZ)}
    recv(rm.at[2], m_id)
    recv(rp.at[3], p_id)
    sb1[...] = (tb1[z].astype(F32) + rp[3].astype(F32) + rm[2].astype(F32)).astype(BF16)
    x_ids = {k: send(sb1.at[wrap(x + k, NX)], rx1.at[x], "x", k) for k in range(1, NX)}
    branch1 = sb1[x].astype(F32)
    for k in range(1, NX):
        src = wrap(x - k, NX)
        recv(rx1.at[src], x_ids[k])
        branch1 = branch1 + rx1[src].astype(F32)
    branch0 = sb0[z].astype(F32)
    for k in range(1, NZ):
        src = wrap(z - k, NZ)
        recv(rz0.at[src], z_ids[k])
        branch0 = branch0 + rz0[src].astype(F32)
    labeled = (state[...] + jnp.concatenate([branch0, branch1], axis=0)).astype(BF16)
    labeled_ref[...] = labeled

    prx[x] = nt(jnp.broadcast_to(rw_ref[...], (16, HD)), labeled)[0:8]
    x_ids = {k: send(prx.at[x], prx.at[x], "x", k) for k in range(1, NX)}
    for k in range(1, NX):
        recv(prx.at[wrap(x - k, NX)], x_ids[k])
    prz[z] = (prx[0] + prx[1]) + (prx[2] + prx[3])
    z_ids = {k: send(prz.at[z], prz.at[z], "z", k) for k in range(1, NZ)}
    for k in range(1, NZ):
        recv(prz.at[wrap(z - k, NZ)], z_ids[k])
    total = prz[0]
    for i in range(1, NZ):
        total = total + prz[i]
    reward_ref[...] = total[0:1]

    for copy, cond in sent:
        if cond is None:
            copy.wait_send()
        else:
            pl.when(cond)(copy.wait_send)


def per_device(
    queries,
    keys,
    values,
    documents,
    residual,
    labels,
    out_weight,
    norm_gain,
    gate_weight,
    up_weight,
    down_weight,
    reward_weight,
):
    vmem = pl.BlockSpec(memory_space=pltpu.VMEM)
    hbm = pl.BlockSpec(memory_space=pl.ANY)
    smem = pl.BlockSpec(memory_space=pltpu.SMEM)
    attended, labeled, reward = pl.pallas_call(
        body,
        out_shape=(
            jax.ShapeDtypeStruct((1, TOK, D), BF16),
            jax.ShapeDtypeStruct((ROWS, HD), BF16),
            jax.ShapeDtypeStruct((1, ROWS), F32),
        ),
        in_specs=[vmem, hbm, hbm, vmem, vmem, smem, hbm, vmem, vmem, vmem, hbm, vmem],
        out_specs=(vmem, vmem, vmem),
        scratch_shapes=[
            pltpu.VMEM((8, TOK, KVH * HD), BF16),
            pltpu.VMEM((8, TOK, KVH * HD), BF16),
            pltpu.VMEM((8, 8, TOK), jnp.int32),
            pltpu.VMEM((8, 512, HD), BF16),
            pltpu.VMEM((8, 512, 2 * FFL), BF16),
            pltpu.VMEM((8, FFL, 512), BF16),
            pltpu.VMEM((TOK, 8 * TOK), F32),
            pltpu.VMEM((KVH, 4 * LAB, HD), BF16),
            pltpu.VMEM((KVH, 4 * LAB, HD), F32),
            pltpu.VMEM((NX, NZ, 16, 1024), BF16),
            pltpu.VMEM((NZ, NX, 16, 1024), BF16),
            pltpu.VMEM((NZ, NX, LAB, HD), F32),
            pltpu.VMEM((NZ, NX, LAB, HD), F32),
            pltpu.VMEM((NX, NZ, LAB, HD), F32),
            pltpu.VMEM((ROWS, HD), F32),
            pltpu.VMEM((NX, NZ, 144, HD), BF16),
            pltpu.VMEM((NZ, NX, 144, HD), BF16),
            pltpu.VMEM((ROWS, 2 * FFL), F32),
            pltpu.VMEM((NX, NZ, 128, HD), BF16),
            pltpu.VMEM((NX, NZ, 128, HD), BF16),
            pltpu.VMEM((NZ, 128, HD), BF16),
            pltpu.VMEM((NZ, 128, HD), BF16),
            pltpu.VMEM((NZ, NX, 128, HD), BF16),
            pltpu.VMEM((4, NX, 128, HD), BF16),
            pltpu.VMEM((3, NX, 128, HD), BF16),
            pltpu.VMEM((3, NX, 128, HD), BF16),
            pltpu.VMEM((2, NX, 128, HD), BF16),
            pltpu.VMEM((NX, 128, HD), BF16),
            pltpu.VMEM((NX, 128, HD), BF16),
            pltpu.VMEM((NX, 8, ROWS), F32),
            pltpu.VMEM((NZ, 8, ROWS), F32),
            pltpu.SemaphoreType.DMA((NSEM,)),
            pltpu.SemaphoreType.DMA((NSEM,)),
            pltpu.SemaphoreType.DMA((4,)),
        ],
        compiler_params=pltpu.CompilerParams(
            collective_id=0, has_side_effects=True, vmem_limit_bytes=56 * 1024 * 1024
        ),
        name="layer",
    )(
        queries,
        keys,
        values,
        documents,
        residual,
        labels,
        out_weight,
        norm_gain.reshape(1, HD),
        gate_weight,
        up_weight,
        down_weight,
        reward_weight.reshape(1, HD),
    )
    return attended, labeled, reward.reshape(ROWS)


def solution(mesh):
    return jax.shard_map(
        per_device,
        mesh=mesh,
        in_specs=(
            P(("grp", "tp"), "ctx", None),
            P(("grp", "tp"), "ctx", None),
            P(("grp", "tp"), "ctx", None),
            P(("grp", "tp"), "ctx"),
            P(("grp", "tp"), "ctx", None),
            P(("grp", "tp"), "ctx"),
            P("ctx", ("grp", "tp")),
            P(("grp", "tp")),
            P("ctx", ("grp", "tp")),
            P("ctx", ("grp", "tp")),
            P(("grp", "tp"), "ctx"),
            P(("grp", "tp")),
        ),
        out_specs=(P(("grp", "tp"), "ctx", None), P("ctx", ("grp", "tp")), P("ctx")),
        check_vma=False,
    )
```

time: 920 us -> 168 us (0.18)
  waiting for transfers between devices: 692 us -> 0 us
  Pallas kernels: 0 us -> 159 us
  blocking collectives: 154 us -> 0 us
  matrix products: 31.3 us -> 0 us
  between operations: 14.3 us -> 0.66 us
  local copies, waits for them, and re-layouts: 19.3 us -> 6.64 us
    all_gather x9 -> x0, waiting for transfers between devices: 532 us -> none  [the longest x1 147 us: per_device(): lax.all_gather(picked, ('grp', 'tp'), axis=0, tiled=True)]
    pallas_call x0 -> x1, Pallas kernels: none -> 159 us  [per_device(): pl.pallas_call(body, out_shape=(jax.ShapeDtypeStruct((1, TOK, D), BF16),...]
    reduce_scatter x1 -> x0, waiting for transfers between devices: 157 us -> none  [per_device(): lax.psum_scatter(terms, ('grp', 'tp'), scatter_dimension=1, tiled=True)]
    psum x2 -> x0, blocking collectives: 146 us -> none  [the longest x1 74.5 us: per_device(): squares = lax.psum(jnp.sum(state * state, axis=-1), ('grp', 'tp'))]
    dot_general x6 -> x0, matrix products: 31.3 us -> none  [the longest x1 10.5 us: per_device(): jnp.einsum('kgrs,skd->kgrd', weight.astype(jnp.bfloat16), value_rows, pre...]
  transfers between devices with their start and end apart: 10 -> 0, of which waited for: 9 -> 0; matrix products, arithmetic and copies ran while one was open for 4% -> 0% of each run, Pallas kernels for 0% -> 0%
where the time goes in v1:
time: 168 us; the launch traced here: 166 us
  Pallas kernels  159 us (95%)
  local copies, waits for them, and re-layouts  6.64 us (4%)
    pallas_call x1, Pallas kernels, per_device(): pl.pallas_call(body, out_shape=(jax.ShapeDtypeStruct((1, TOK, D), BF16),...  159 us
    unnamed x11, local copies, waits for them, and re-layouts  6.64 us

profile of v1, /device:TPU:24, one launch (start us, length us, event | category | flops | bytes accessed | tf_op | source)
XLA Modules:
  0.0 165.9 jit_solution(6452016412837098777)
XLA Ops:
  0.6 0.0 copy-start
  0.6 2.1 %copy.15.gate_ref = bf16[512,448]{1,0:T(8,128)(2,1)} copy(bf16[512,448]{0,1:T(8,128)(2,1)} %param.20) | data formatting | bytes 917504 | tf_op args[8]
  2.7 0.0 copy-done
  2.7 1.0 copy.16.up_ref
  3.7 158.6 %layer.1 = (bf16[1,128,4096]{2,1,0:T(8,128)(2,1)}, bf16[256,128]{1,0:T(8,128)(2,1)}, f32[1,256]{1,0:T(1,128)}) custom-call(bf16[1,128,4096]{2,1,0:T(8,128)(2,1)} %q_ref.1, bf16[1,128,1024]{2,1,0:T(8,128)(2,1)} %k_ref.1, bf16[1,128,1024]{2,1,0:T(8,128)(2,1)} %v_ref.1, s32[1,128]{1,0:T(1,128)} %doc_ref.1, bf16[1,128,4096]{2,1,0:T(8,128)(2,1)} %res_ref.1, ...), custom_call_target="tpu_custom_call" | custom-call | tf_op jit(solution)/shard_map/layer/pallas_call | solution.py:527
  162.3 0.0 copy-start.1
  162.3 2.3 %copy.20 = bf16[1,128,4096]{2,1,0:T(8,128)(2,1)} copy(bf16[1,128,4096]{2,1,0:T(8,128)(2,1)} %get-tuple-element.12) | data formatting | bytes 2097152
  164.6 0.0 copy-done.1
  164.6 0.0 copy-start.2
  164.6 0.6 copy.21
  165.3 0.0 copy-done.2
  165.3 0.6 copy.22
Async XLA Ops:
  0.6 2.1 %copy-start = (bf16[512,448]{0,1:T(8,128)(2,1)S(1)}, bf16[512,448]{0,1:T(8,128)(2,1)}, u32[]{:S(2)}) copy-start(bf16[512,448]{0,1:T(8,128)(2,1)} %param.21) | copy-start | bytes 1376260
  162.3 2.3 %copy-start.1 = (bf16[256,128]{1,0:T(8,128)(2,1)S(1)}, bf16[256,128]{1,0:T(8,128)(2,1)}, u32[]{:S(2)}) copy-start(bf16[256,128]{1,0:T(8,128)(2,1)} %get-tuple-element.13) | copy-start | bytes 196612
  164.6 0.7 copy-start.2

commit v2 on v1

v2 whole, which is shorter than its diff:
```python
import functools
import math

import jax
import jax.numpy as jnp
from jax import lax
from jax.experimental import pallas as pl
from jax.experimental.pallas import tpu as pltpu
from jax.sharding import PartitionSpec as P

MESH = pl.DeviceIdType.MESH
NX, NY, NZ = 4, 4, 8
D, H, KVH, HD, FF = 4096, 32, 8, 128, 14336
TOK, LAB = 128, 8
ROWS = 256
FFL = 448
F32, BF16 = jnp.float32, jnp.bfloat16
SCALE2 = HD**-0.5 * math.log2(math.e)
NSEM = 288
PLAN = {
    "start": (
        ("own", "out"),
        ("own", "gu"),
        ("own", "down"),
    ),
    "keys": (
        ("first", "out", "up", 0),
        ("first", "out", "dn", 1),
        ("first", "out", "up", 1),
        ("first", "out", "dn", 0),
        ("first", "gu", "up", 0),
        ("first", "gu", "dn", 1),
    ),
    "first1": (
        ("turn", "out", "up", 0),
        ("turn", "out", "dn", 1),
        ("first", "gu", "up", 1),
        ("first", "gu", "dn", 0),
    ),
    "first3": (
        ("share", "out", "up", 1),
        ("share", "out", "dn", 0),
    ),
    "first5": (
        ("turn", "gu", "up", 0),
        ("turn", "gu", "dn", 1),
        ("share", "out", "far", 0),
        ("share", "out", "far", 1),
        ("first", "down", "up", 0),
        ("first", "down", "dn", 1),
    ),
    "second4": (
        ("turn", "down", "up", 0),
        ("turn", "down", "dn", 1),
        ("first", "down", "up", 1),
        ("first", "down", "dn", 0),
    ),
    "second5": (
        ("share", "gu", "dn", 0),
        ("share", "gu", "up", 1),
        ("share", "gu", "far", 1),
        ("share", "gu", "far", 0),
    ),
    "down": (
        ("share", "down", "up", 1),
        ("share", "down", "dn", 0),
        ("share", "down", "far", 1),
        ("share", "down", "far", 0),
    ),
}
A1 = {0: (0,), 5: (1, 2)}
A2 = {0: (3,), 5: (4, 5)}
A3 = {"start": (6,), "end": (7,)}

def block_of(col):
    grp, tp = col // 2, col % 2
    return (grp // NZ) * 2 + tp, grp % NZ


def nt(a, b):
    return lax.dot_general(a, b, (((1,), (1,)), ((), ())), preferred_element_type=F32)


def body(
    q_ref,
    k_ref,
    v_ref,
    doc_ref,
    res_ref,
    lab_ref,
    ow_ref,
    gain_ref,
    gate_ref,
    up_ref,
    dn_ref,
    rw_ref,
    att_ref,
    labeled_ref,
    reward_ref,
    kbuf,
    vbuf,
    dbuf,
    ow,
    gu,
    dn,
    bias,
    qlab,
    plab,
    a0,
    a1,
    bsrc,
    bz,
    bx,
    state,
    s0,
    s1,
    acc,
    tb0,
    rx0,
    sb0,
    rz0,
    tb1,
    rp,
    rm,
    sp,
    sm,
    sb1,
    rx1,
    prx,
    prz,
    ss,
    rs,
    ls,
):
    ctx, grp, tp = lax.axis_index("ctx"), lax.axis_index("grp"), lax.axis_index("tp")
    y, core = ctx // 2, ctx % 2
    x, z = (grp // NZ) * 2 + tp, grp % NZ
    other = y * 2 + 1 - core

    def wrap(v, n):
        return lax.rem(v + n, n)

    def dev(axis, k):
        if axis == "y":
            return {"ctx": wrap(y + k, NY) * 2 + core}
        if axis == "core":
            return {"ctx": other}
        if axis == "ctx":
            return {"ctx": wrap(ctx + k, 2 * NY)}
        if axis == "z":
            return {"grp": (x // 2) * NZ + wrap(z + k, NZ)}
        there = wrap(x + k, NX)
        return {"grp": (there // 2) * NZ + z, "tp": there % 2}

    ids = iter(range(NSEM))
    sent = []

    def send(src, dst, axis, k, cond=None, when=None):
        i = next(ids)
        copy = pltpu.make_async_remote_copy(
            src_ref=src,
            dst_ref=dst,
            send_sem=ss.at[i],
            recv_sem=rs.at[i],
            device_id=dev(axis, k),
            device_id_type=MESH,
        )
        if cond is None:
            copy.start()
        else:
            pl.when(cond)(copy.start)
        sent.append((copy, cond))
        return i

    def recv(dst, i):
        pltpu.make_async_remote_copy(
            src_ref=dst,
            dst_ref=dst,
            send_sem=ss.at[i],
            recv_sem=rs.at[i],
            device_id={"ctx": other},
            device_id_type=MESH,
        ).wait_recv()

    barrier = pltpu.get_barrier_semaphore()
    partners = [("core", 1)] + [("y", k) for k in range(1, NY)]
    partners += [("x", k) for k in range(1, NX)]
    partners += [("z", k) for k in range(1, NZ)]
    for axis, k in partners:
        pl.semaphore_signal(barrier, inc=1, device_id=dev(axis, k), device_id_type=MESH)

    local = [
        pltpu.make_async_copy(k_ref.at[0], kbuf.at[ctx], ls.at[0]),
        pltpu.make_async_copy(v_ref.at[0], vbuf.at[ctx], ls.at[1]),
        pltpu.make_async_copy(ow_ref, ow.at[ctx], ls.at[2]),
        pltpu.make_async_copy(dn_ref, dn.at[ctx], ls.at[3]),
        pltpu.make_async_copy(gate_ref, gu.at[ctx, pl.ds(0, FFL)], ls.at[4]),
        pltpu.make_async_copy(up_ref, gu.at[ctx, pl.ds(FFL, FFL)], ls.at[5]),
    ]
    for copy in local:
        copy.start()
    dbuf[ctx] = jnp.broadcast_to(doc_ref[...], (8, TOK))
    for j in range(1, 2 * NY):

        @pl.when(j > ctx)
        def _():
            kbuf[j] = jnp.zeros_like(kbuf[j])
            vbuf[j] = jnp.zeros_like(vbuf[j])
            dbuf[j] = jnp.zeros_like(dbuf[j])
    pl.semaphore_wait(barrier, len(partners))

    def halves_of(ref):
        half = ref.shape[0] // 2
        return ref.at[pl.ds(0, half)], ref.at[pl.ds(half, half)]

    kv_ids = {k: [] for k in (1, 3, 2)}
    kv_own = []
    for src, buf in ((dbuf.at[ctx], dbuf), (k_ref.at[0], kbuf), (v_ref.at[0], vbuf)):
        for k in (1, 3, 2):
            kv_ids[k].append(send(src, buf.at[ctx], "y", k, y + k < NY, y - k >= 0))
        kv_own.append(send(src, buf.at[ctx], "core", 1, core == 0, core == 1))

    weights = {
        "out": (halves_of(ow_ref), ow, {}),
        "gu": ((gate_ref, up_ref), gu, {}),
        "down": (halves_of(dn_ref), dn, {}),
    }

    def w_piece(buf, k, h, c):
        return halves_of(buf.at[wrap(y + k, NY) * 2 + c])[h]

    def w_act(act, which, name="", h=0):
        parts, buf, got = weights[which]
        if act == "first":
            slot = halves_of(buf.at[ctx])[h]
            got[name, h] = send(parts[h], slot, "y", 1 if name == "up" else -1)
        elif act == "own":
            for h in (0, 1):
                got["own", h] = send(parts[h], halves_of(buf.at[ctx])[h], "core", 1)
        else:
            k = {"up": -1, "dn": 1, "far": 2}[name]
            ref = w_piece(buf, k, h, core)
            recv(ref, got[name, h])
            if act == "turn":
                got["far", h] = send(ref, ref, "y", -k)
            got["core", k, h] = send(ref, ref, "core", 1)

    def w_done(which):
        _, buf, got = weights[which]
        for h in (0, 1):
            recv(halves_of(buf.at[other])[h], got["own", h])
        for k in (-1, 1, 2):
            for h in (0, 1):
                recv(w_piece(buf, k, h, 1 - core), got["core", k, h])

    def plan(point):
        for entry in PLAN.get(point, ()):
            w_act(*entry)

    plan("start")
    row_of = lax.broadcasted_iota(jnp.int32, (LAB, TOK), 0)
    lane_of = lax.broadcasted_iota(jnp.int32, (LAB, TOK), 1)
    lab_col = jnp.zeros((LAB, TOK), jnp.int32)
    for r in range(LAB):
        lab_col = jnp.where(row_of == r, lab_ref[0, r], lab_col)
    chosen = (lane_of == lab_col).astype(F32)
    pick = chosen.astype(BF16)
    my_doc = doc_ref[...].astype(F32)
    q_lab = jnp.dot(pick, q_ref[0], preferred_element_type=F32).astype(BF16)
    for k in range(KVH):
        qlab[k] = jnp.concatenate(
            [q_lab[:, (4 * k + g) * HD : (4 * k + g + 1) * HD] for g in range(4)], axis=0
        )
    base = jnp.dot(pick, res_ref[0], preferred_element_type=F32)
    reward_row = jnp.broadcast_to(rw_ref[...].astype(F32), (LAB, HD))
    for col in range(NX * NZ):
        bx_, bz_ = block_of(col)
        bsrc[bz_, bx_, 0:LAB] = base[:, col * HD : (col + 1) * HD]
        bsrc[bz_, bx_, LAB:] = reward_row
    bz[z] = bsrc[z]
    bz_ids = {k: send(bsrc.at[wrap(z + k, NZ)], bz.at[z], "z", k) for k in range(1, NZ)}
    for copy in local:
        copy.wait()

    def attend(q, keys, values, add):
        score = nt(q, keys) * SCALE2 + add
        top = jnp.max(score, axis=1, keepdims=True)
        weight = jnp.exp2(score - top)
        total = jnp.sum(weight, axis=1, keepdims=True)
        out = jnp.dot(weight.astype(BF16), values, preferred_element_type=F32) / total
        return out

    for k in range(1, NZ):
        recv(bz.at[wrap(z - k, NZ)], bz_ids[k])
    bx[x] = bz[:, x]
    bx_ids = {k: send(bz.at[:, wrap(x + k, NX)], bx.at[x], "x", k) for k in range(1, NX)}
    bufs = (dbuf, kbuf, vbuf)
    kv_core = {}

    def kv_turn():
        for b, buf in enumerate(bufs):
            for k in (1, 3, 2):
                ok = y - k >= 0
                ref = buf.at[wrap(y - k, NY) * 2 + core]
                pl.when(ok)(functools.partial(recv, ref, kv_ids[k][b]))
                kv_core[k, b] = send(ref, ref, "core", 1, ok, ok)

    def kv_done():
        for b, buf in enumerate(bufs):
            for k in (1, 3, 2):
                ref = buf.at[wrap(y - k, NY) * 2 + 1 - core]
                pl.when(y - k >= 0)(functools.partial(recv, ref, kv_core[k, b]))
            pl.when(core == 1)(functools.partial(recv, buf.at[other], kv_own[b]))

    kv_turn()
    plan("keys")
    kv_done()

    key_doc = jnp.concatenate([dbuf[j][0:1] for j in range(2 * NY)], axis=1).astype(F32)
    key_pos = lax.broadcasted_iota(jnp.int32, (1, 2 * NY * TOK), 1)
    lab_doc = jnp.sum(chosen * my_doc, axis=1, keepdims=True)
    keep = (key_pos <= lab_col[:, 0:1] + ctx * TOK) & (key_doc == lab_doc)
    lab_bias = jnp.concatenate([jnp.where(keep, 0.0, -1e30)] * 4, axis=0)

    def head(buf, k):
        return buf[:, :, pl.ds(k * HD, HD)].reshape(2 * NY * TOK, HD)

    for k in range(KVH):
        plab[k] = attend(qlab[k], head(kbuf, k), head(vbuf, k), lab_bias)
    halves = []
    for h in range(2):
        rows = []
        for sub in range(2):
            pieces = []
            for k in (4 * h + 2 * sub, 4 * h + 2 * sub + 1):
                pieces += [plab[k, g * LAB : (g + 1) * LAB] for g in range(4)]
            rows.append(jnp.concatenate(pieces, axis=1))
        halves.append(jnp.concatenate(rows, axis=0).astype(BF16))
    a0[x, z] = halves[0]
    a1[z, x] = halves[1]

    def gather(b0, b1, between):
        def block(k):
            return b0.at[x, wrap(z + k, NZ)]

        def group(k, i):
            return b1.at[wrap(z + k, NZ), pl.ds(i * (NX // 2), NX // 2)]

        def spread(k):
            return {j: send(block(k), block(k), "x", j) for j in (1, 3, 2)}

        own = b1.at[z, x]
        x_ids = {k: send(own, own, "x", k) for k in (1, 3, 2)}
        z_ids = {k: send(block(0), block(0), "z", k) for k in (1, 7, 2, 6, 3, 5, 4)}
        far = {0: spread(0)}
        between(0)
        for k in (1, 3, 2):
            recv(b1.at[z, wrap(x - k, NX)], x_ids[k])
        up = [send(group(0, i), group(0, i), "z", 1) for i in (0, 1)]
        down = [send(group(0, i), group(0, i), "z", -1) for i in (1, 0)][::-1]
        for step in range(1, 5):
            between(step)
            for k in (-step, step) if step < 4 else (4,):
                recv(block(k), z_ids[-k % NZ])
                far[k] = spread(k)
            for i in (0, 1):
                if step < 4 or i == 0:
                    recv(group(-step, i), up[i])
                    if step < 3 or (step == 3 and i == 0):
                        up[i] = send(group(-step, i), group(-step, i), "z", 1)
                j = 1 - i
                if step < 4 or j == 1:
                    recv(group(step, j), down[j])
                    if step < 3 or (step == 3 and j == 1):
                        down[j] = send(group(step, j), group(step, j), "z", -1)
        between(5)
        for k, ids_k in far.items():
            for j in (1, 3, 2):
                recv(b0.at[wrap(x - j, NX), wrap(z + k, NZ)], ids_k[j])

    def make_bias():
        doc_col = jnp.transpose(jnp.broadcast_to(my_doc, (TOK, TOK)))[:, 0:1]
        my_pos = lax.broadcasted_iota(jnp.int32, (TOK, 1), 0) + ctx * TOK
        full = (key_pos <= my_pos) & (key_doc == doc_col)
        bias[...] = jnp.where(full, 0.0, -1e30)

    def att_heads(start, stop):
        def one(k, carry):
            lanes = pl.ds(pl.multiple_of(k * HD, HD), HD)
            keys = kbuf[:, :, lanes].reshape(2 * NY * TOK, HD)
            values = vbuf[:, :, lanes].reshape(2 * NY * TOK, HD)
            for g in range(4):
                span = pl.ds(pl.multiple_of((4 * k + g) * HD, HD), HD)
                out = attend(q_ref[0, :, span], keys, values, bias[...])
                att_ref[0, :, span] = out.astype(BF16)
            return carry

        lax.fori_loop(start, stop, one, 0)

    plan("first")
    def between_first(step):
        plan("first%d" % step)
        if step == 0:
            make_bias()
            for k in range(1, NX):
                recv(bx.at[wrap(x - k, NX)], bx_ids[k])
        for k in A1.get(step, ()):
            att_heads(k, k + 1)

    gather(a0, a1, between_first)
    plan("out")
    w_done("out")

    whole = ow[...].reshape(D, HD)
    quarter = D // 4
    flat = {0: a0[...].reshape(-1, quarter), 1: a1[...].reshape(-1, quarter)}
    proj = []
    for h in range(2):
        wide = jnp.concatenate(
            [whole[(2 * h + s) * quarter : (2 * h + s + 1) * quarter] for s in range(2)], axis=1
        )
        proj.append(jnp.dot(flat[h], wide, preferred_element_type=F32))
    for col in range(NX * NZ):
        bx_, bz_ = block_of(col)
        r0, r1 = (bx_ * NZ + bz_) * 16, (bz_ * NX + bx_) * 16
        state[col * LAB : (col + 1) * LAB] = (
            bx[bx_, bz_, 0:LAB]
            + (proj[0][r0 : r0 + 8, :HD] + proj[0][r0 + 8 : r0 + 16, HD:])
            + (proj[1][r1 : r1 + 8, :HD] + proj[1][r1 + 8 : r1 + 16, HD:])
        )

    gain = gain_ref[...].astype(F32)
    sixteen = lax.broadcasted_iota(jnp.int32, (16, HD), 0)
    for h, put in ((0, s0.at[x, z]), (1, s1.at[z, x])):
        part = state[h * 128 : (h + 1) * 128]
        put[0:128] = (part * gain).astype(BF16)
        square = jnp.sum(jnp.transpose(part * part), axis=0, keepdims=True)
        top = square.astype(BF16).astype(F32)
        mid = (square - top).astype(BF16).astype(F32)
        low = square - top - mid
        put[128:144] = jnp.where(
            sixteen == 0,
            top,
            jnp.where(sixteen == 1, mid, jnp.where(sixteen == 2, low, 0.0)),
        ).astype(BF16)

    plan("second")

    def between_second(step):
        plan("second%d" % step)
        for k in A2.get(step, ()):
            att_heads(k, k + 1)

    gather(s0, s1, between_second)
    plan("gu")
    w_done("gu")

    def inv_rms(buf):
        total = jnp.zeros((16, HD), F32)
        for i in range(buf.shape[0]):
            for j in range(buf.shape[1]):
                total = total + buf[i, j, 128:144].astype(F32)
        line = jnp.sum(total, axis=0, keepdims=True)
        col = jnp.transpose(jnp.broadcast_to(line, (128, 128)))
        return lax.rsqrt(col / D + 1e-5)

    scale = jnp.concatenate([inv_rms(s0), inv_rms(s1)], axis=0)
    acc[...] = jnp.zeros_like(acc)
    for c in range(2 * NY):
        pieces = []
        for col in range(4 * c, 4 * c + 4):
            bx_, bz_ = block_of(col)
            pieces.append(jnp.concatenate([s0[bx_, bz_, 0:128], s1[bz_, bx_, 0:128]], axis=0))
        acc[...] += nt(jnp.concatenate(pieces, axis=1), gu[c])
    scale = jnp.concatenate([scale] * 4, axis=1)[:, :FFL]
    gate = acc[:, :FFL] * scale
    up = acc[:, FFL:] * scale
    hidden = (gate / (1.0 + jnp.exp(-gate)) * up).astype(BF16)

    plan("down")
    w_done("down")
    own_reward = jnp.broadcast_to(rw_ref[...], (16, HD))
    high = state[...].astype(BF16)
    part_reward = nt(own_reward, high) + nt(own_reward, (state[...] - high.astype(F32)).astype(BF16))
    for c in range(2 * NY):
        terms = jnp.dot(hidden, dn[c], preferred_element_type=F32).astype(BF16)
        line = [bx[block_of(4 * c + i) + (slice(LAB, None),)] for i in range(4)]
        line = jnp.concatenate(line, axis=1)
        part_reward = part_reward + nt(jnp.concatenate([line, line], axis=0).astype(BF16), terms)
        for i in range(4):
            bx_, bz_ = block_of(4 * c + i)
            cols = terms[:, i * HD : (i + 1) * HD]
            tb0[bx_, bz_] = cols[:128]
            tb1[bz_, bx_] = cols[128:]

    lo, hi = pl.ds(0, NX // 2), pl.ds(NX // 2, NX // 2)
    chains = {
        "up_lo": (1, lo, 4, rp, sp),
        "dn_hi": (-1, hi, 4, rm, sm),
        "up_hi": (1, hi, 3, rp, sp),
        "dn_lo": (-1, lo, 3, rm, sm),
    }
    hop = {}
    for name, (k, part, count, got, _) in chains.items():
        hop[name] = send(tb1.at[wrap(z + k * count, NZ), part], got.at[0, part], "z", k)
    x_ids = {}
    for d in (4, 3, -3, 2, -2, 1, -1, 0):
        there = wrap(z + d, NZ)
        for k in (1, 3, 2):
            x_ids[d, k] = send(tb0.at[wrap(x + k, NX), there], rx0.at[x, there], "x", k)
    prx[x] = part_reward[0:8]
    rx_ids = {k: send(prx.at[x], prx.at[x], "x", k) for k in range(1, NX)}
    for k in A3.get("start", ()):
        att_heads(k, k + 1)
    z_ids = {}

    def add_x(d):
        there = wrap(z + d, NZ)
        total = tb0[x, there].astype(F32)
        for k in (1, 3, 2):
            src = wrap(x - k, NX)
            recv(rx0.at[src, there], x_ids[d, k])
            total = total + rx0[src, there].astype(F32)
        return total

    def pass_on(d):
        there = wrap(z + d, NZ)
        sb0[there] = add_x(d).astype(BF16)
        z_ids[d % NZ] = send(sb0.at[there], rz0.at[z], "z", d)

    for step in range(3):
        for name, (k, part, count, got, out) in chains.items():
            if step + 1 < count:
                recv(got.at[step, part], hop[name])
                own = tb1[wrap(z + k * (count - 1 - step), NZ), part]
                out[step, part] = (got[step, part].astype(F32) + own.astype(F32)).astype(BF16)
                hop[name] = send(out.at[step, part], got.at[step + 1, part], "z", k)
        for d in ((4, 3), (-3, 2), (-2, 1))[step]:
            pass_on(d)
    pass_on(-1)
    for k in range(1, NX):
        recv(prx.at[wrap(x - k, NX)], rx_ids[k])
    prz[z] = (prx[0] + prx[1]) + (prx[2] + prx[3])
    rz_ids = {k: send(prz.at[z], prz.at[z], "z", k) for k in range(1, NZ)}
    for name, (k, part, count, got, _) in chains.items():
        recv(got.at[count - 1, part], hop[name])
    for part, last_up, last_down in ((lo, 3, 2), (hi, 2, 3)):
        pair = rp[last_up, part].astype(F32) + rm[last_down, part].astype(F32)
        sb1[part] = (tb1[z, part].astype(F32) + pair).astype(BF16)
    far_ids = {k: send(sb1.at[wrap(x + k, NX)], rx1.at[x], "x", k) for k in range(1, NX)}
    for k in A3.get("end", ()):
        att_heads(k, k + 1)
    branch1 = sb1[x].astype(F32)
    for k in range(1, NX):
        src = wrap(x - k, NX)
        recv(rx1.at[src], far_ids[k])
        branch1 = branch1 + rx1[src].astype(F32)
    branch0 = add_x(0)
    for k in range(1, NZ):
        src = wrap(z - k, NZ)
        recv(rz0.at[src], z_ids[k])
        branch0 = branch0 + rz0[src].astype(F32)
    labeled = (state[...] + jnp.concatenate([branch0, branch1], axis=0)).astype(BF16)
    labeled_ref[...] = labeled
    for k in range(1, NZ):
        recv(prz.at[wrap(z - k, NZ)], rz_ids[k])
    total = prz[0]
    for i in range(1, NZ):
        total = total + prz[i]
    reward_ref[...] = total[0:1]

    for copy, cond in sent:
        if cond is None:
            copy.wait_send()
        else:
            pl.when(cond)(copy.wait_send)


def per_device(
    queries,
    keys,
    values,
    documents,
    residual,
    labels,
    out_weight,
    norm_gain,
    gate_weight,
    up_weight,
    down_weight,
    reward_weight,
):
    vmem = pl.BlockSpec(memory_space=pltpu.VMEM)
    hbm = pl.BlockSpec(memory_space=pl.ANY)
    smem = pl.BlockSpec(memory_space=pltpu.SMEM)
    attended, labeled, reward = pl.pallas_call(
        body,
        out_shape=(
            jax.ShapeDtypeStruct((1, TOK, D), BF16),
            jax.ShapeDtypeStruct((ROWS, HD), BF16),
            jax.ShapeDtypeStruct((1, ROWS), F32),
        ),
        in_specs=[vmem, hbm, hbm, vmem, vmem, smem, hbm, vmem, hbm, hbm, hbm, vmem],
        out_specs=(vmem, vmem, vmem),
        scratch_shapes=[
            pltpu.VMEM((8, TOK, KVH * HD), BF16),
            pltpu.VMEM((8, TOK, KVH * HD), BF16),
            pltpu.VMEM((8, 8, TOK), jnp.int32),
            pltpu.VMEM((8, 512, HD), BF16),
            pltpu.VMEM((8, 2 * FFL, 512), BF16),
            pltpu.VMEM((8, FFL, 512), BF16),
            pltpu.VMEM((TOK, 8 * TOK), F32),
            pltpu.VMEM((KVH, 4 * LAB, HD), BF16),
            pltpu.VMEM((KVH, 4 * LAB, HD), F32),
            pltpu.VMEM((NX, NZ, 16, 1024), BF16),
            pltpu.VMEM((NZ, NX, 16, 1024), BF16),
            pltpu.VMEM((NZ, NX, 2 * LAB, HD), F32),
            pltpu.VMEM((NZ, NX, 2 * LAB, HD), F32),
            pltpu.VMEM((NX, NZ, 2 * LAB, HD), F32),
            pltpu.VMEM((ROWS, HD), F32),
            pltpu.VMEM((NX, NZ, 144, HD), BF16),
            pltpu.VMEM((NZ, NX, 144, HD), BF16),
            pltpu.VMEM((ROWS, 2 * FFL), F32),
            pltpu.VMEM((NX, NZ, 128, HD), BF16),
            pltpu.VMEM((NX, NZ, 128, HD), BF16),
            pltpu.VMEM((NZ, 128, HD), BF16),
            pltpu.VMEM((NZ, 128, HD), BF16),
            pltpu.VMEM((NZ, NX, 128, HD), BF16),
            pltpu.VMEM((4, NX, 128, HD), BF16),
            pltpu.VMEM((4, NX, 128, HD), BF16),
            pltpu.VMEM((3, NX, 128, HD), BF16),
            pltpu.VMEM((3, NX, 128, HD), BF16),
            pltpu.VMEM((NX, 128, HD), BF16),
            pltpu.VMEM((NX, 128, HD), BF16),
            pltpu.VMEM((NX, 8, ROWS), F32),
            pltpu.VMEM((NZ, 8, ROWS), F32),
            pltpu.SemaphoreType.DMA((NSEM,)),
            pltpu.SemaphoreType.DMA((NSEM,)),
            pltpu.SemaphoreType.DMA((6,)),
        ],
        compiler_params=pltpu.CompilerParams(
            collective_id=0, has_side_effects=True, vmem_limit_bytes=56 * 1024 * 1024
        ),
        name="layer",
    )(
        queries,
        keys,
        values,
        documents,
        residual,
        labels,
        out_weight,
        norm_gain.reshape(1, HD),
        gate_weight.T,
        up_weight.T,
        down_weight,
        reward_weight.reshape(1, HD),
    )
    return attended, labeled, reward.reshape(ROWS)


def solution(mesh):
    return jax.shard_map(
        per_device,
        mesh=mesh,
        in_specs=(
            P(("grp", "tp"), "ctx", None),
            P(("grp", "tp"), "ctx", None),
            P(("grp", "tp"), "ctx", None),
            P(("grp", "tp"), "ctx"),
            P(("grp", "tp"), "ctx", None),
            P(("grp", "tp"), "ctx"),
            P("ctx", ("grp", "tp")),
            P(("grp", "tp")),
            P("ctx", ("grp", "tp")),
            P("ctx", ("grp", "tp")),
            P(("grp", "tp"), "ctx"),
            P(("grp", "tp")),
        ),
        out_specs=(P(("grp", "tp"), "ctx", None), P("ctx", ("grp", "tp")), P("ctx")),
        check_vma=False,
    )
```

time: 168 us -> 131 us (0.78)
  Pallas kernels: 159 us -> 126 us
  local copies, waits for them, and re-layouts: 6.64 us -> 3.55 us
    pallas_call x1, Pallas kernels: 159 us -> 126 us  [per_device(): pl.pallas_call(body, out_shape=(jax.ShapeDtypeStruct((1, TOK, D), BF16),...]
    unnamed x11 -> x7, local copies, waits for them, and re-layouts: 6.64 us -> 3.55 us
where the time goes in v2:
time: 131 us; the launch traced here: 130 us
  Pallas kernels  126 us (96%)
  local copies, waits for them, and re-layouts  3.55 us (3%)
    pallas_call x1, Pallas kernels, per_device(): pl.pallas_call(body, out_shape=(jax.ShapeDtypeStruct((1, TOK, D), BF16),...  126 us
    unnamed x7, local copies, waits for them, and re-layouts  3.55 us

profile of v2, /device:TPU:24, one launch (start us, length us, event | category | flops | bytes accessed | tf_op | source)
XLA Modules:
  0.0 129.9 jit_solution(7657550248178532584)
XLA Ops:
  0.6 125.7 %layer.1 = (bf16[1,128,4096]{2,1,0:T(8,128)(2,1)}, bf16[256,128]{1,0:T(8,128)(2,1)}, f32[1,256]{1,0:T(1,128)}) custom-call(bf16[1,128,4096]{2,1,0:T(8,128)(2,1)} %q_ref.1, bf16[1,128,1024]{2,1,0:T(8,128)(2,1)} %k_ref.1, bf16[1,128,1024]{2,1,0:T(8,128)(2,1)} %v_ref.1, s32[1,128]{1,0:T(1,128)} %doc_ref.1, bf16[1,128,4096]{2,1,0:T(8,128)(2,1)} %res_ref.1, ...), custom_call_target="tpu_custom_call" | custom-call | tf_op jit(solution)/shard_map/layer/pallas_call | solution.py:596
  126.3 0.0 copy-start
  126.3 2.3 %copy.18 = bf16[1,128,4096]{2,1,0:T(8,128)(2,1)} copy(bf16[1,128,4096]{2,1,0:T(8,128)(2,1)} %get-tuple-element.12) | data formatting | bytes 2097152
  128.6 0.0 copy-done
  128.6 0.0 copy-start.1
  128.6 0.6 copy.19
  129.3 0.0 copy-done.1
  129.3 0.6 copy.20
Async XLA Ops:
  126.3 2.3 %copy-start = (bf16[256,128]{1,0:T(8,128)(2,1)S(1)}, bf16[256,128]{1,0:T(8,128)(2,1)}, u32[]{:S(2)}) copy-start(bf16[256,128]{1,0:T(8,128)(2,1)} %get-tuple-element.13) | copy-start | bytes 196612
  128.6 0.7 copy-start.1

commit v3 on v2

--- a/solution.py
+++ b/solution.py
@@ -13,6 +13,9 @@
 D, H, KVH, HD, FF = 4096, 32, 8, 128, 14336
 TOK, LAB = 128, 8
 ROWS = 256
+R0, R1 = 144, 112
+AHEAD = 3
+C0, C1 = 1280, 768
 FFL = 448
 F32, BF16 = jnp.float32, jnp.bfloat16
 SCALE2 = HD**-0.5 * math.log2(math.e)
@@ -82,11 +85,11 @@
 
 
 def body(
-    q_ref,
+    q_hbm,
     k_ref,
     v_ref,
     doc_ref,
-    res_ref,
+    res_hbm,
     lab_ref,
     ow_ref,
     gain_ref,
@@ -97,6 +100,8 @@
     att_ref,
     labeled_ref,
     reward_ref,
+    q_ref,
+    res_ref,
     kbuf,
     vbuf,
     dbuf,
@@ -190,6 +195,8 @@
         pl.semaphore_signal(barrier, inc=1, device_id=dev(axis, k), device_id_type=MESH)
 
     local = [
+        pltpu.make_async_copy(q_hbm, q_ref, ls.at[6]),
+        pltpu.make_async_copy(res_hbm, res_ref, ls.at[7]),
         pltpu.make_async_copy(k_ref.at[0], kbuf.at[ctx], ls.at[0]),
         pltpu.make_async_copy(v_ref.at[0], vbuf.at[ctx], ls.at[1]),
         pltpu.make_async_copy(ow_ref, ow.at[ctx], ls.at[2]),
@@ -200,13 +207,6 @@
     for copy in local:
         copy.start()
     dbuf[ctx] = jnp.broadcast_to(doc_ref[...], (8, TOK))
-    for j in range(1, 2 * NY):
-
-        @pl.when(j > ctx)
-        def _():
-            kbuf[j] = jnp.zeros_like(kbuf[j])
-            vbuf[j] = jnp.zeros_like(vbuf[j])
-            dbuf[j] = jnp.zeros_like(dbuf[j])
     pl.semaphore_wait(barrier, len(partners))
 
     def halves_of(ref):
@@ -258,6 +258,13 @@
             w_act(*entry)
 
     plan("start")
+    for j in range(1, 2 * NY):
+
+        @pl.when(j > ctx)
+        def _():
+            kbuf[j] = jnp.zeros_like(kbuf[j])
+            vbuf[j] = jnp.zeros_like(vbuf[j])
+            dbuf[j] = jnp.zeros_like(dbuf[j])
     row_of = lax.broadcasted_iota(jnp.int32, (LAB, TOK), 0)
     lane_of = lax.broadcasted_iota(jnp.int32, (LAB, TOK), 1)
     lab_col = jnp.zeros((LAB, TOK), jnp.int32)
@@ -266,6 +273,8 @@
     chosen = (lane_of == lab_col).astype(F32)
     pick = chosen.astype(BF16)
     my_doc = doc_ref[...].astype(F32)
+    for copy in local[:2]:
+        copy.wait()
     q_lab = jnp.dot(pick, q_ref[0], preferred_element_type=F32).astype(BF16)
     for k in range(KVH):
         qlab[k] = jnp.concatenate(
@@ -279,7 +288,7 @@
         bsrc[bz_, bx_, LAB:] = reward_row
     bz[z] = bsrc[z]
     bz_ids = {k: send(bsrc.at[wrap(z + k, NZ)], bz.at[z], "z", k) for k in range(1, NZ)}
-    for copy in local:
+    for copy in local[2:]:
         copy.wait()
 
     def attend(q, keys, values, add):
@@ -325,21 +334,25 @@
     def head(buf, k):
         return buf[:, :, pl.ds(k * HD, HD)].reshape(2 * NY * TOK, HD)
 
-    for k in range(KVH):
-        plab[k] = attend(qlab[k], head(kbuf, k), head(vbuf, k), lab_bias)
-    halves = []
-    for h in range(2):
+    def lab_heads(start, stop):
+        for k in range(start, stop):
+            plab[k] = attend(qlab[k], head(kbuf, k), head(vbuf, k), lab_bias)
+
+    def lab_part(first, wide):
         rows = []
-        for sub in range(2):
-            pieces = []
-            for k in (4 * h + 2 * sub, 4 * h + 2 * sub + 1):
-                pieces += [plab[k, g * LAB : (g + 1) * LAB] for g in range(4)]
+        for top in (first, first + wide // 2):
+            pieces = [plab[h // 4, h % 4 * LAB : h % 4 * LAB + LAB] for h in range(top, top + wide // 2)]
             rows.append(jnp.concatenate(pieces, axis=1))
-        halves.append(jnp.concatenate(rows, axis=0).astype(BF16))
-    a0[x, z] = halves[0]
-    a1[z, x] = halves[1]
-
-    def gather(b0, b1, between):
+        return jnp.concatenate(rows, axis=0).astype(BF16)
+
+    split = 2 * C0 // HD
+    lab_heads(split // 4, KVH)
+    a1[z, x] = lab_part(split, 2 * C1 // HD)
+    a1_ids = {k: send(a1.at[z, x], a1.at[z, x], "x", k) for k in (1, 3, 2)}
+    lab_heads(0, split // 4)
+    a0[x, z] = lab_part(0, 2 * C0 // HD)
+
+    def gather(b0, b1, between, x_ids=None):
         def block(k):
             return b0.at[x, wrap(z + k, NZ)]
 
@@ -350,8 +363,9 @@
             return {j: send(block(k), block(k), "x", j) for j in (1, 3, 2)}
 
         own = b1.at[z, x]
-        x_ids = {k: send(own, own, "x", k) for k in (1, 3, 2)}
-        z_ids = {k: send(block(0), block(0), "z", k) for k in (1, 7, 2, 6, 3, 5, 4)}
+        if x_ids is None:
+            x_ids = {k: send(own, own, "x", k) for k in (1, 3, 2)}
+        z_ids = {k: send(block(0), block(0), "z", k) for k in (1, 7, 2, 6)}
         far = {0: spread(0)}
         between(0)
         for k in (1, 3, 2):
@@ -360,6 +374,8 @@
         down = [send(group(0, i), group(0, i), "z", -1) for i in (1, 0)][::-1]
         for step in range(1, 5):
             between(step)
+            if step == 1:
+                z_ids.update({k: send(block(0), block(0), "z", k) for k in (3, 5, 4)})
             for k in (-step, step) if step < 4 else (4,):
                 recv(block(k), z_ids[-k % NZ])
                 far[k] = spread(k)
@@ -407,19 +423,16 @@
         for k in A1.get(step, ()):
             att_heads(k, k + 1)
 
-    gather(a0, a1, between_first)
+    gather(a0, a1, between_first, a1_ids)
     plan("out")
     w_done("out")
 
     whole = ow[...].reshape(D, HD)
-    quarter = D // 4
-    flat = {0: a0[...].reshape(-1, quarter), 1: a1[...].reshape(-1, quarter)}
     proj = []
-    for h in range(2):
-        wide = jnp.concatenate(
-            [whole[(2 * h + s) * quarter : (2 * h + s + 1) * quarter] for s in range(2)], axis=1
-        )
-        proj.append(jnp.dot(flat[h], wide, preferred_element_type=F32))
+    for buf, first, wide in ((a0, 0, C0), (a1, 2 * C0, C1)):
+        pair = [whole[first + i * wide : first + (i + 1) * wide] for i in range(2)]
+        pair = jnp.concatenate(pair, axis=1)
+        proj.append(jnp.dot(buf[...].reshape(-1, wide), pair, preferred_element_type=F32))
     for col in range(NX * NZ):
         bx_, bz_ = block_of(col)
         r0, r1 = (bx_ * NZ + bz_) * 16, (bz_ * NX + bx_) * 16
@@ -431,18 +444,18 @@
 
     gain = gain_ref[...].astype(F32)
     sixteen = lax.broadcasted_iota(jnp.int32, (16, HD), 0)
-    for h, put in ((0, s0.at[x, z]), (1, s1.at[z, x])):
+    scaled = (state[...] * gain).astype(BF16)
+    s1[z, x] = scaled[R0:]
+    s0[x, z, 0:R0] = scaled[:R0]
+    sums = jnp.zeros((16, HD), F32)
+    for h in range(2):
         part = state[h * 128 : (h + 1) * 128]
-        put[0:128] = (part * gain).astype(BF16)
         square = jnp.sum(jnp.transpose(part * part), axis=0, keepdims=True)
         top = square.astype(BF16).astype(F32)
         mid = (square - top).astype(BF16).astype(F32)
-        low = square - top - mid
-        put[128:144] = jnp.where(
-            sixteen == 0,
-            top,
-            jnp.where(sixteen == 1, mid, jnp.where(sixteen == 2, low, 0.0)),
-        ).astype(BF16)
+        for i, value in enumerate((top, mid, square - top - mid)):
+            sums = jnp.where(sixteen == 3 * h + i, value, sums)
+    s0[x, z, R0:] = sums.astype(BF16)
 
     plan("second")
 
@@ -455,22 +468,21 @@
     plan("gu")
     w_done("gu")
 
-    def inv_rms(buf):
-        total = jnp.zeros((16, HD), F32)
-        for i in range(buf.shape[0]):
-            for j in range(buf.shape[1]):
-                total = total + buf[i, j, 128:144].astype(F32)
-        line = jnp.sum(total, axis=0, keepdims=True)
-        col = jnp.transpose(jnp.broadcast_to(line, (128, 128)))
-        return lax.rsqrt(col / D + 1e-5)
-
-    scale = jnp.concatenate([inv_rms(s0), inv_rms(s1)], axis=0)
+    total = jnp.zeros((16, HD), F32)
+    for i in range(NX):
+        for j in range(NZ):
+            total = total + s0[i, j, R0:].astype(F32)
+    scale = []
+    for h in range(2):
+        line = jnp.sum(total[3 * h : 3 * h + 3], axis=0, keepdims=True)
+        scale.append(lax.rsqrt(jnp.transpose(jnp.broadcast_to(line, (128, 128))) / D + 1e-5))
+    scale = jnp.concatenate(scale, axis=0)
     acc[...] = jnp.zeros_like(acc)
     for c in range(2 * NY):
         pieces = []
         for col in range(4 * c, 4 * c + 4):
             bx_, bz_ = block_of(col)
-            pieces.append(jnp.concatenate([s0[bx_, bz_, 0:128], s1[bz_, bx_, 0:128]], axis=0))
+            pieces.append(jnp.concatenate([s0[bx_, bz_, 0:R0], s1[bz_, bx_]], axis=0))
         acc[...] += nt(jnp.concatenate(pieces, axis=1), gu[c])
     scale = jnp.concatenate([scale] * 4, axis=1)[:, :FFL]
     gate = acc[:, :FFL] * scale
@@ -490,8 +502,8 @@
         for i in range(4):
             bx_, bz_ = block_of(4 * c + i)
             cols = terms[:, i * HD : (i + 1) * HD]
-            tb0[bx_, bz_] = cols[:128]
-            tb1[bz_, bx_] = cols[128:]
+            tb0[bx_, bz_] = cols[:R0]
+            tb1[bz_, bx_] = cols[R0:]
 
     lo, hi = pl.ds(0, NX // 2), pl.ds(NX // 2, NX // 2)
     chains = {
@@ -504,10 +516,15 @@
     for name, (k, part, count, got, _) in chains.items():
         hop[name] = send(tb1.at[wrap(z + k * count, NZ), part], got.at[0, part], "z", k)
     x_ids = {}
-    for d in (4, 3, -3, 2, -2, 1, -1, 0):
+    order = (4, 3, -3, 2, -2, 1, -1, 0)
+
+    def send_x(d):
         there = wrap(z + d, NZ)
         for k in (1, 3, 2):
             x_ids[d, k] = send(tb0.at[wrap(x + k, NX), there], rx0.at[x, there], "x", k)
+
+    for d in order[:AHEAD]:
+        send_x(d)
     prx[x] = part_reward[0:8]
     rx_ids = {k: send(prx.at[x], prx.at[x], "x", k) for k in range(1, NX)}
     for k in A3.get("start", ()):
@@ -521,6 +538,8 @@
             src = wrap(x - k, NX)
             recv(rx0.at[src, there], x_ids[d, k])
             total = total + rx0[src, there].astype(F32)
+        if d in order[:-AHEAD]:
+            send_x(order[order.index(d) + AHEAD])
         return total
 
     def pass_on(d):
@@ -600,9 +619,11 @@
             jax.ShapeDtypeStruct((ROWS, HD), BF16),
             jax.ShapeDtypeStruct((1, ROWS), F32),
         ),
-        in_specs=[vmem, hbm, hbm, vmem, vmem, smem, hbm, vmem, hbm, hbm, hbm, vmem],
+        in_specs=[hbm, hbm, hbm, vmem, hbm, smem, hbm, vmem, hbm, hbm, hbm, vmem],
         out_specs=(vmem, vmem, vmem),
         scratch_shapes=[
+            pltpu.VMEM((1, TOK, D), BF16),
+            pltpu.VMEM((1, TOK, D), BF16),
             pltpu.VMEM((8, TOK, KVH * HD), BF16),
             pltpu.VMEM((8, TOK, KVH * HD), BF16),
             pltpu.VMEM((8, 8, TOK), jnp.int32),
@@ -612,31 +633,31 @@
             pltpu.VMEM((TOK, 8 * TOK), F32),
             pltpu.VMEM((KVH, 4 * LAB, HD), BF16),
             pltpu.VMEM((KVH, 4 * LAB, HD), F32),
-            pltpu.VMEM((NX, NZ, 16, 1024), BF16),
-            pltpu.VMEM((NZ, NX, 16, 1024), BF16),
+            pltpu.VMEM((NX, NZ, 16, C0), BF16),
+            pltpu.VMEM((NZ, NX, 16, C1), BF16),
             pltpu.VMEM((NZ, NX, 2 * LAB, HD), F32),
             pltpu.VMEM((NZ, NX, 2 * LAB, HD), F32),
             pltpu.VMEM((NX, NZ, 2 * LAB, HD), F32),
             pltpu.VMEM((ROWS, HD), F32),
-            pltpu.VMEM((NX, NZ, 144, HD), BF16),
-            pltpu.VMEM((NZ, NX, 144, HD), BF16),
+            pltpu.VMEM((NX, NZ, R0 + 16, HD), BF16),
+            pltpu.VMEM((NZ, NX, R1, HD), BF16),
             pltpu.VMEM((ROWS, 2 * FFL), F32),
-            pltpu.VMEM((NX, NZ, 128, HD), BF16),
-            pltpu.VMEM((NX, NZ, 128, HD), BF16),
-            pltpu.VMEM((NZ, 128, HD), BF16),
-            pltpu.VMEM((NZ, 128, HD), BF16),
-            pltpu.VMEM((NZ, NX, 128, HD), BF16),
-            pltpu.VMEM((4, NX, 128, HD), BF16),
-            pltpu.VMEM((4, NX, 128, HD), BF16),
-            pltpu.VMEM((3, NX, 128, HD), BF16),
-            pltpu.VMEM((3, NX, 128, HD), BF16),
-            pltpu.VMEM((NX, 128, HD), BF16),
-            pltpu.VMEM((NX, 128, HD), BF16),
+            pltpu.VMEM((NX, NZ, R0, HD), BF16),
+            pltpu.VMEM((NX, NZ, R0, HD), BF16),
+            pltpu.VMEM((NZ, R0, HD), BF16),
+            pltpu.VMEM((NZ, R0, HD), BF16),
+            pltpu.VMEM((NZ, NX, R1, HD), BF16),
+            pltpu.VMEM((4, NX, R1, HD), BF16),
+            pltpu.VMEM((4, NX, R1, HD), BF16),
+            pltpu.VMEM((3, NX, R1, HD), BF16),
+            pltpu.VMEM((3, NX, R1, HD), BF16),
+            pltpu.VMEM((NX, R1, HD), BF16),
+            pltpu.VMEM((NX, R1, HD), BF16),
             pltpu.VMEM((NX, 8, ROWS), F32),
             pltpu.VMEM((NZ, 8, ROWS), F32),
             pltpu.SemaphoreType.DMA((NSEM,)),
             pltpu.SemaphoreType.DMA((NSEM,)),
-            pltpu.SemaphoreType.DMA((6,)),
+            pltpu.SemaphoreType.DMA((8,)),
         ],
         compiler_params=pltpu.CompilerParams(
             collective_id=0, has_side_effects=True, vmem_limit_bytes=56 * 1024 * 1024

time: 131 us -> 127 us (0.969)
  Pallas kernels: 126 us -> 122 us
    pallas_call x1, Pallas kernels: 126 us -> 122 us  [per_device(): pl.pallas_call(body, out_shape=(jax.ShapeDtypeStruct((1, TOK, D), BF16),...]
where the time goes in v3:
time: 127 us
  Pallas kernels  122 us (96%)
  local copies, waits for them, and re-layouts  3.55 us (3%)
    pallas_call x1, Pallas kernels, per_device(): pl.pallas_call(body, out_shape=(jax.ShapeDtypeStruct((1, TOK, D), BF16),...  122 us
    unnamed x7, local copies, waits for them, and re-layouts  3.55 us

profile of v3, /device:TPU:24, one launch (start us, length us, event | category | flops | bytes accessed | tf_op | source)
XLA Modules:
  0.0 126.6 jit_solution(1115916472961907885)
XLA Ops:
  0.6 122.4 %layer.1 = (bf16[1,128,4096]{2,1,0:T(8,128)(2,1)}, bf16[256,128]{1,0:T(8,128)(2,1)}, f32[1,256]{1,0:T(1,128)}) custom-call(bf16[1,128,4096]{2,1,0:T(8,128)(2,1)} %q_hbm.1, bf16[1,128,1024]{2,1,0:T(8,128)(2,1)} %k_ref.1, bf16[1,128,1024]{2,1,0:T(8,128)(2,1)} %v_ref.1, s32[1,128]{1,0:T(1,128)} %doc_ref.1, bf16[1,128,4096]{2,1,0:T(8,128)(2,1)} %res_hbm.1, ...), custom_call_target="tpu_custom_call" | custom-call | tf_op jit(solution)/shard_map/layer/pallas_call | solution.py:615
  123.0 0.0 copy-start
  123.0 2.3 %copy.18 = bf16[1,128,4096]{2,1,0:T(8,128)(2,1)} copy(bf16[1,128,4096]{2,1,0:T(8,128)(2,1)} %get-tuple-element.12) | data formatting | bytes 2097152
  125.4 0.0 copy-done
  125.4 0.0 copy-start.1
  125.4 0.6 copy.19
  126.0 0.0 copy-done.1
  126.0 0.6 copy.20
Async XLA Ops:
  123.0 2.3 %copy-start = (bf16[256,128]{1,0:T(8,128)(2,1)S(1)}, bf16[256,128]{1,0:T(8,128)(2,1)}, u32[]{:S(2)}) copy-start(bf16[256,128]{1,0:T(8,128)(2,1)} %get-tuple-element.13) | copy-start | bytes 196612
  125.4 0.7 copy-start.1

commit v4 on v3

--- a/solution.py
+++ b/solution.py
@@ -13,7 +13,7 @@
 D, H, KVH, HD, FF = 4096, 32, 8, 128, 14336
 TOK, LAB = 128, 8
 ROWS = 256
-R0, R1 = 144, 112
+R0, R1 = 160, 96
 AHEAD = 3
 C0, C1 = 1280, 768
 FFL = 448
@@ -51,12 +51,12 @@
         ("share", "out", "far", 1),
         ("first", "down", "up", 0),
         ("first", "down", "dn", 1),
+        ("first", "down", "up", 1),
+        ("first", "down", "dn", 0),
     ),
     "second4": (
         ("turn", "down", "up", 0),
         ("turn", "down", "dn", 1),
-        ("first", "down", "up", 1),
-        ("first", "down", "dn", 0),
     ),
     "second5": (
         ("share", "gu", "dn", 0),

time: 127 us -> 126 us (level)
  no operation moved by 1% of the time
where the time goes in v4:
time: 126 us; the launch traced here: 125 us
  Pallas kernels  121 us (96%)
  local copies, waits for them, and re-layouts  3.55 us (3%)
    pallas_call x1, Pallas kernels, per_device(): pl.pallas_call(body, out_shape=(jax.ShapeDtypeStruct((1, TOK, D), BF16),...  121 us
    unnamed x7, local copies, waits for them, and re-layouts  3.55 us

profile of v4, /device:TPU:24, one launch (start us, length us, event | category | flops | bytes accessed | tf_op | source)
XLA Modules:
  0.0 125.4 jit_solution(4139407926734943799)
XLA Ops:
  0.6 121.2 %layer.1 = (bf16[1,128,4096]{2,1,0:T(8,128)(2,1)}, bf16[256,128]{1,0:T(8,128)(2,1)}, f32[1,256]{1,0:T(1,128)}) custom-call(bf16[1,128,4096]{2,1,0:T(8,128)(2,1)} %q_hbm.1, bf16[1,128,1024]{2,1,0:T(8,128)(2,1)} %k_ref.1, bf16[1,128,1024]{2,1,0:T(8,128)(2,1)} %v_ref.1, s32[1,128]{1,0:T(1,128)} %doc_ref.1, bf16[1,128,4096]{2,1,0:T(8,128)(2,1)} %res_hbm.1, ...), custom_call_target="tpu_custom_call" | custom-call | tf_op jit(solution)/shard_map/layer/pallas_call | solution.py:615
  121.8 0.0 copy-start
  121.8 2.3 %copy.18 = bf16[1,128,4096]{2,1,0:T(8,128)(2,1)} copy(bf16[1,128,4096]{2,1,0:T(8,128)(2,1)} %get-tuple-element.12) | data formatting | bytes 2097152
  124.2 0.0 copy-done
  124.2 0.0 copy-start.1
  124.2 0.6 copy.19
  124.8 0.0 copy-done.1
  124.8 0.6 copy.20
Async XLA Ops:
  121.8 2.3 %copy-start = (bf16[256,128]{1,0:T(8,128)(2,1)S(1)}, bf16[256,128]{1,0:T(8,128)(2,1)}, u32[]{:S(2)}) copy-start(bf16[256,128]{1,0:T(8,128)(2,1)} %get-tuple-element.13) | copy-start | bytes 196612
  124.2 0.7 copy-start.1
